TPU v7x, 32 devices: a whole 2x2x4 slice. The times are simulated.
32 devices in a mesh: trainer: 8 (over y, x, core), depth: 4 (over z).
Axes of the slice: x: 2, y: 2, z: 4, core: 2. Of those that a mesh axis runs over, the one named last changes fastest.
Arguments:
- noise: bfloat16 [8, 16, 64, 256], P('trainer', 'depth'), may hold values from -6 to 6
- gen_weight: float32 [8, 331776], P('trainer', 'depth'), may hold values from -0.15625 to 0.15625
- gen_momentum: float32 [8, 331776], P('trainer', 'depth'), may hold values from -6 to 6
- disc_weight: bfloat16 [8, 8, 128, 64], P('trainer'), may hold values from -0.25 to 0.25
- score_weight: float32 [8, 128], P('trainer'), may hold values from -0.5 to 0.5
- pairing: int32 [8], replicated, may hold values from 0 to 7, as said below
- flags: int32 [8], replicated, may hold values from 0 to 1, as said below
Outputs:
- generated: bfloat16 [8, 16, 64, 256], P('trainer', 'depth')
- new_weight: float32 [8, 331776], P('trainer', 'depth')
- new_momentum: float32 [8, 331776], P('trainer', 'depth')
Inputs may be any that keep to these rules, and one draw needn't show every extreme that they name: pairing is a perfect matching: pairing[pairing[i]] == i and pairing[i] != i for every trainer. `flags`: in every matched pair exactly one trainer has flag 1.
All inputs are finite; a program needn't handle non-finite values.
Results may differ from a plain program's by a relative error of at most 0.013.
Values may be sent and summed in bfloat16 or wider, within the bound.
A program may use at most 64 MiB of HBM per device.

v0:
```python
import jax
import jax.numpy as jnp
from jax import lax
from jax.sharding import PartitionSpec as P

Y = 2
X = 128


momentum_decay = 0.9
step_length = 0.01


def extended(block, sides, width):
    for axis, dim in sides:
        count = lax.axis_size(axis)
        forward = [(i, i + 1) for i in range(count - 1)]
        backward = [(target, source) for source, target in forward]
        low = lax.ppermute(
            lax.slice_in_dim(block, block.shape[dim] - width, None, axis=dim), axis, forward
        )
        high = lax.ppermute(lax.slice_in_dim(block, 0, width, axis=dim), axis, backward)
        block = jnp.concatenate([low, block, high], axis=dim)
    return block


def framed_copies(padded):
    breadth = X
    cells = padded.shape[2]
    framed = jnp.pad(padded, ((0, 0), (0, 0), (breadth + 1, breadth + 1)))
    column = (jnp.arange(cells + 2 * breadth + 2, dtype=jnp.int32) - breadth - 1) % breadth
    left_copy = jnp.where(
        (column == breadth - 1)[None, None, :], jnp.zeros((), framed.dtype), framed
    )
    right_copy = jnp.where((column == 0)[None, None, :], jnp.zeros((), framed.dtype), framed)
    return (left_copy, framed, right_copy)


def stacked_window(copies, read_y, cells):
    breadth = X
    parts_list = []
    for read_x in range(3):
        begin = read_y * breadth + read_x
        parts_list.append(copies[read_x][:, :, begin : begin + cells])
    return jnp.concatenate(parts_list, axis=1)


def group_kernel(layer):
    channels = layer.shape[-1]
    cube = layer.reshape(3, 3, 3, channels, channels)
    return cube.transpose(0, 1, 3, 2, 4).reshape(3, 3, channels, 3 * channels)


def flip_kernel(layer):
    channels = layer.shape[-1]
    cube = layer.reshape(3, 3, 3, channels, channels)[::-1, ::-1, ::-1].swapaxes(3, 4)
    return cube.transpose(0, 1, 3, 2, 4).reshape(3, 3, channels, 3 * channels)


def convolve_grouped(padded, grouped):
    planes, cells = (padded.shape[0] - 2, padded.shape[2])
    copies = framed_copies(padded)
    summed = jnp.zeros((planes, grouped.shape[2], cells), jnp.float32)
    for read_y in range(3):
        window = stacked_window(copies, read_y, cells)
        for read_z in range(3):
            summed = summed + jnp.einsum(
                "oj,zjs->zos",
                grouped[read_z, read_y],
                window[read_z : read_z + planes],
                preferred_element_type=jnp.float32,
            )
    return summed


def convolve(padded, layer):
    return convolve_grouped(padded, group_kernel(layer))


def convolve_back(padded, layer):
    return convolve_grouped(padded, flip_kernel(layer))


def kernel_grad(gradient, padded):
    planes, channels_out, cells = gradient.shape
    channels_in = padded.shape[1]
    copies = framed_copies(padded)
    rows_list = []
    for read_z in range(3):
        row_list = []
        for read_y in range(3):
            window = stacked_window(copies, read_y, cells)
            row_list.append(
                jnp.einsum(
                    "zos,zjs->oj",
                    gradient,
                    window[read_z : read_z + planes],
                    preferred_element_type=jnp.float32,
                )
            )
        rows_list.append(jnp.stack(row_list))
    grouped = jnp.stack(rows_list)
    return (
        grouped.reshape(3, 3, channels_out, 3, channels_in)
        .transpose(0, 1, 3, 2, 4)
        .reshape(27, channels_out, channels_in)
    )


def gelu_back(inputs, upstream):
    return jax.vjp(jax.nn.gelu, inputs)[1](upstream)[0]


def widen_back(gradient):
    return extended(gradient, (("depth", 0),), 1)


def widen_forward(volume):
    return extended(volume, (("depth", 0),), 1)


def critic_grad(generated, disc_kernel, score_vector):
    planes, channels, cells = generated.shape
    blocks = generated.reshape(planes // 2, 2, channels, Y // 2, 2, X // 2, 2)
    kernel_cube = disc_kernel.reshape(2, 2, 2, disc_kernel.shape[1], channels)
    response = jnp.einsum(
        "abdoc,zacybxd->zoyx", kernel_cube, blocks, preferred_element_type=jnp.float32
    )
    features = jax.nn.gelu(response)
    scores = jnp.sum(score_vector[None, :, None, None] * features, axis=1)
    slope = -jax.nn.sigmoid(-scores)
    upstream = gelu_back(response, slope[:, None] * score_vector[None, :, None, None]).astype(
        jnp.bfloat16
    )
    spread = jnp.einsum(
        "abdoc,zoyx->zacybxd", kernel_cube, upstream, preferred_element_type=jnp.float32
    )
    return spread.reshape(planes, channels, cells)


def on_device(noise, gen_weight, gen_momentum, disc_weight, score_weight, pairing, flags):
    trainer_rank = lax.axis_index("trainer")
    partner = pairing[trainer_rank]
    keeper = flags[trainer_rank] == 1
    trainer_count = lax.axis_size("trainer")
    own_pair = jnp.concatenate([gen_weight, gen_momentum], axis=0)
    slot_ids = jnp.arange(trainer_count, dtype=jnp.int32)
    outgoing = jnp.where((slot_ids == partner)[:, None, None], own_pair[None], 0.0)
    incoming = lax.all_to_all(
        outgoing.astype(jnp.bfloat16), "trainer", split_axis=0, concat_axis=0, tiled=True
    ).astype(outgoing.dtype)
    arrived = lax.dynamic_index_in_dim(incoming, partner, 0, keepdims=False)
    other_weight, other_moment = (arrived[0:1], arrived[1:2])
    chosen_weight = jnp.where(keeper, gen_weight, other_weight)
    chosen_momentum = jnp.where(keeper, gen_momentum, other_moment)
    channels = noise.shape[2]
    all_kernels = lax.all_gather(chosen_weight.astype(jnp.bfloat16), "depth", axis=1, tiled=True)
    layers = all_kernels.reshape(3, 27, channels, channels)
    latent = noise[0]
    latent_pad = widen_forward(latent)
    first_pre = convolve(latent_pad, layers[0])
    first_act_pad = widen_forward(jax.nn.gelu(first_pre).astype(jnp.bfloat16))
    second_pre = convolve(first_act_pad, layers[1])
    second_act_pad = widen_forward(jax.nn.gelu(second_pre).astype(jnp.bfloat16))
    third_pre = convolve(second_act_pad, layers[2])
    output_f = jnp.tanh(third_pre)
    generated = output_f.astype(jnp.bfloat16)
    gen_grad = critic_grad(generated, disc_weight[0], score_weight[0])
    third_grad = (gen_grad * (1.0 - output_f * output_f)).astype(jnp.bfloat16)
    grad_three = kernel_grad(third_grad, second_act_pad)
    second_back = convolve_back(widen_back(third_grad), layers[2])
    second_grad = gelu_back(second_pre, second_back).astype(jnp.bfloat16)
    grad_two = kernel_grad(second_grad, first_act_pad)
    first_back = convolve_back(widen_back(second_grad), layers[1])
    first_grad = gelu_back(first_pre, first_back).astype(jnp.bfloat16)
    grad_one = kernel_grad(first_grad, latent_pad)
    local_grad = jnp.concatenate(
        [grad_one.reshape(-1), grad_two.reshape(-1), grad_three.reshape(-1)]
    )
    share_len = gen_weight.shape[1]
    grad_whole = lax.psum(local_grad.astype(jnp.bfloat16), "depth").astype(jnp.float32)
    grad_share = lax.dynamic_slice_in_dim(
        grad_whole, lax.axis_index("depth") * share_len, share_len, 0
    )
    new_momentum = momentum_decay * chosen_momentum + grad_share[None, :]
    new_weight = chosen_weight - step_length * new_momentum
    return (generated[None], new_weight, new_momentum)


def solution(mesh):
    placed = (
        P("trainer", "depth", None, None),
        P("trainer", "depth"),
        P("trainer", "depth"),
        P("trainer", None, None, None),
        P("trainer", None),
        P(),
        P(),
    )
    return jax.shard_map(
        on_device,
        mesh=mesh,
        in_specs=placed,
        out_specs=(P("trainer", "depth", None, None), P("trainer", "depth"), P("trainer", "depth")),
        check_vma=False,
    )
```

profile of v0, /device:TPU:0, one launch (start us, length us, event | category | flops | bytes accessed | tf_op | source)
XLA Modules:
  0.0 229.6 jit_solution(1383116195382707316)
XLA Ops:
  7.2 1.3 dynamic_slice.14
  9.1 1.7 pad_maximum_fusion
  10.8 3.1 %select_convert_fusion = bf16[8,2,82944]{2,1,0:T(2,128)(2,1)} fusion(pred[8]{0:T(512)(128)(4,1)S(1)} %iota_compare_fusion.2, bf16[2,82944]{1,0:T(2,128)(2,1)S(1)} %pad_maximum_fusion), kind=kLoop, calls=%fused_computation | loop fusion | flops 1327104 | bytes 2985992 | tf_op jit(solution)/shard_map/convert_element_type | solution.py:150
  13.9 5.3 %all-to-all-start = ((bf16[8,2,82944]{2,1,0:T(2,128)(2,1)}), bf16[8,2,82944]{2,1,0:T(2,128)(2,1)}, u32[]{:S(2)}, u32[]{:S(2)}) async-start(bf16[8,2,82944]{2,1,0:T(2,128)(2,1)} %select_convert_fusion), calls=%async_computation | async-start | bytes 5308416 | tf_op jit(solution)/shard_map/all_to_all | solution.py:149
  19.2 4.2 %collective-permute-start = (bf16[1,64,256]{2,1,0:T(8,128)(2,1)S(1)}, bf16[1,64,256]{2,1,0:T(8,128)(2,1)S(1)}, u32[]{:S(2)}, u32[]{:S(2)}) collective-permute-start(bf16[1,64,256]{2,1,0:T(8,128)(2,1)S(1)} %get-tuple-element.71), channel_id=1, source_target_pairs={{0,1},{1,2},{2,3},{4,5},{5,6},{6,7},{8,9},{9,10},{10,11},{12,13},{... | collective-permute-start | bytes 98312 | tf_op jit(solution)/shard_map/ppermute | solution.py:19
  23.4 1.3 collective-permute-start.1
  28.0 1.2 collective-permute-done.1
  30.2 21.7 %all-to-all-done = bf16[8,2,82944]{2,1,0:T(2,128)(2,1)} async-done(((bf16[8,2,82944]{2,1,0:T(2,128)(2,1)}), bf16[8,2,82944]{2,1,0:T(2,128)(2,1)}, u32[]{:S(2)}, u32[]{:S(2)}) %all-to-all-start) | async-done | bytes 2654240 | tf_op jit(solution)/shard_map/all_to_all | solution.py:149
  51.9 1.2 dynamic-slice_convert_fusion
  53.1 0.9 copy-done.9
  54.3 25.9 %all_gather.3 = bf16[1,331776]{1,0:T(2,128)(2,1)S(1)} all-gather(bf16[1,82944]{1,0:T(2,128)(2,1)S(1)} %fusion.171), channel_id=1, replica_groups=mesh['trainer'=8,'depth'=4] {'depth'}, dimensions={1}, use_global_device_ids=true | all-gather | bytes 829440 | tf_op jit(solution)/shard_map/all_gather | solution.py:157
  80.2 4.4 %slice_reduce_fusion.2 = (bf16[110592]{0:T(1024)(128)(2,1)}, bf16[110592]{0:T(1024)(128)(2,1)S(1)}, bf16[110592]{0:T(1024)(128)(2,1)S(1)}) fusion(bf16[1,331776]{1,0:T(2,128)(2,1)S(1)} %all_gather.3), kind=kLoop, calls=%fused_computation.152 | loop fusion | bytes 1327104 | tf_op jit(solution)/shard_map/slice | solution.py:165
  86.9 1.0 multiply_convert_fusion.1
  87.9 1.3 collective-permute-start.2
  89.2 1.5 collective-permute-start.3
  91.1 4.0 %collective-permute-done.3 = bf16[1,64,256]{2,1,0:T(8,128)(2,1)S(1)} collective-permute-done((bf16[1,64,256]{2,1,0:T(8,128)(2,1)S(1)}, bf16[1,64,256]{2,1,0:T(8,128)(2,1)S(1)}, u32[]{:S(2)}, u32[]{:S(2)}) %collective-permute-start.3) | collective-permute-done | bytes 32800 | tf_op jit(solution)/shard_map/ppermute | solution.py:22
  97.1 0.8 copy-done.14
  99.1 1.0 multiply_convert_fusion
  101.3 3.9 %collective-permute-start.4 = (bf16[1,64,256]{2,1,0:T(8,128)(2,1)}, bf16[1,64,256]{2,1,0:T(8,128)(2,1)S(1)}, u32[]{:S(2)}, u32[]{:S(2)}) collective-permute-start(bf16[1,64,256]{2,1,0:T(8,128)(2,1)} %get-tuple-element.67), channel_id=1, source_target_pairs={{0,1},{1,2},{2,3},{4,5},{5,6},{6,7},{8,9},{9,10},{10,11},{12,13},{... | collective-permute-start | bytes 98312 | tf_op jit(solution)/shard_map/ppermute | solution.py:19
  105.2 1.3 collective-permute-start.5
  106.5 0.8 rev.7
  107.3 1.1 reshape_squeeze.16
  108.5 0.8 rev.6
  109.3 1.0 copy.284
  110.3 1.1 collective-permute-done.5
  111.4 1.2 broadcast_select_fusion.9
  114.8 0.8 pad_maximum_fusion.9
  117.9 0.8 copy.294
  118.8 1.3 multiply_reduce_fusion
  120.4 1.2 copy.296
  121.6 2.0 copy.297
  123.5 1.1 fusion.136
  124.7 1.3 fusion.31
  128.6 0.7 copy.344
  129.4 0.7 copy.343
  130.1 0.7 copy.342
  130.8 0.7 copy.338
  131.5 0.7 copy.341
  132.2 0.7 copy.337
  132.9 0.7 copy.340
  133.6 0.7 copy.336
  134.4 0.7 copy.339
  135.1 3.5 %collective-permute-start.6 = (bf16[1,64,256]{2,1,0:T(8,128)(2,1)}, bf16[1,64,256]{2,1,0:T(8,128)(2,1)S(1)}, u32[]{:S(2)}, u32[]{:S(2)}) collective-permute-start(bf16[1,64,256]{2,1,0:T(8,128)(2,1)} %get-tuple-element.65), channel_id=1, source_target_pairs={{0,1},{1,2},{2,3},{4,5},{5,6},{6,7},{8,9},{9,10},{10,11},{12,13},{... | collective-permute-start | bytes 98312 | tf_op jit(solution)/shard_map/ppermute | solution.py:19
  138.6 1.3 collective-permute-start.7
  139.9 1.1 maximum_bitcast_fusion.2
  141.0 1.0 copy.345
  142.0 1.3 reshape_reshape.14
  143.2 1.4 collective-permute-done.7
  144.7 1.2 broadcast_select_fusion.8
  148.1 0.8 pad_maximum_fusion.12
  150.9 0.9 fusion.22
  151.8 0.9 fusion.21
  152.7 0.9 fusion.20
  153.8 0.9 fusion.16
  156.3 0.9 copy.334
  157.2 0.9 copy.333
  158.1 0.9 copy.332
  159.7 3.1 %collective-permute-start.8 = (bf16[1,64,256]{2,1,0:T(8,128)(2,1)}, bf16[1,64,256]{2,1,0:T(8,128)(2,1)S(1)}, u32[]{:S(2)}, u32[]{:S(2)}) collective-permute-start(bf16[1,64,256]{2,1,0:T(8,128)(2,1)} %get-tuple-element.63), channel_id=1, source_target_pairs={{0,1},{1,2},{2,3},{4,5},{5,6},{6,7},{8,9},{9,10},{10,11},{12,13},{... | collective-permute-start | bytes 98312 | tf_op jit(solution)/shard_map/ppermute | solution.py:19
  162.8 1.5 collective-permute-start.9
  165.0 3.8 %collective-permute-done.9 = bf16[1,64,256]{2,1,0:T(8,128)(2,1)S(1)} collective-permute-done((bf16[1,64,256]{2,1,0:T(8,128)(2,1)}, bf16[1,64,256]{2,1,0:T(8,128)(2,1)S(1)}, u32[]{:S(2)}, u32[]{:S(2)}) %collective-permute-start.9) | collective-permute-done | bytes 32800 | tf_op jit(solution)/shard_map/ppermute | solution.py:22
  177.2 0.9 pad_maximum_fusion.1
  178.1 41.7 %all-reduce.7.cloned.1.call-done = bf16[331776]{0:T(1024)(128)(2,1)} async-done(((bf16[331776]{0:T(1024)(128)(2,1)}), bf16[331776]{0:T(1024)(128)(2,1)}) %all-reduce.7.cloned.1.call-update) | async-done | bytes 663568 | tf_op jit(solution)/shard_map/psum | solution.py:181
  219.8 0.9 dynamic-slice_convert_fusion.1
  220.8 2.0 multiply_subtract_fusion
  (214 shorter events, 32.2 us)
Async XLA Ops:
  7.2 111.6 %copy-start = (bf16[1,8,128,64]{2,3,1,0:T(8,128)(2,1)S(1)}, bf16[1,8,128,64]{2,3,1,0:T(8,128)(2,1)}, u32[]{:S(2)}) copy-start(bf16[1,8,128,64]{2,3,1,0:T(8,128)(2,1)} %param.10) | copy-start | bytes 393220
  13.9 5.4 %copy-start.25 = (bf16[1,4,64,256]{3,2,1,0:T(8,128)(2,1)S(1)}, bf16[1,4,64,256]{3,2,1,0:T(8,128)(2,1)}, u32[]{:S(2)}) copy-start(bf16[1,4,64,256]{3,2,1,0:T(8,128)(2,1)} %param.7) | copy-start | bytes 393220
  13.9 12.2 %copy-start.36 = (s32[8]{0:T(128)S(1)}, s32[8]{0:T(128)}, u32[]{:S(2)}) copy-start(s32[8]{0:T(128)} %param.13) | copy-start | bytes 100
  13.9 38.0 %all-to-all-start = ((bf16[8,2,82944]{2,1,0:T(2,128)(2,1)}), bf16[8,2,82944]{2,1,0:T(2,128)(2,1)}, u32[]{:S(2)}, u32[]{:S(2)}) async-start(bf16[8,2,82944]{2,1,0:T(2,128)(2,1)} %select_convert_fusion), calls=%async_computation | async-start | bytes 5308416 | tf_op jit(solution)/shard_map/all_to_all | solution.py:149
  19.2 200.6 %all-reduce.7.cloned.1.call-start = ((), (), s32[]{:S(2)}) async-start(), calls=%async_computation.1 | async-start | bytes 1327104 | tf_op jit(solution)/shard_map/psum | solution.py:181
  19.2 8.7 %collective-permute-start = (bf16[1,64,256]{2,1,0:T(8,128)(2,1)S(1)}, bf16[1,64,256]{2,1,0:T(8,128)(2,1)S(1)}, u32[]{:S(2)}, u32[]{:S(2)}) collective-permute-start(bf16[1,64,256]{2,1,0:T(8,128)(2,1)S(1)} %get-tuple-element.71), channel_id=1, source_target_pairs={{0,1},{1,2},{2,3},{4,5},{5,6},{6,7},{8,9},{9,10},{10,11},{12,13},{... | collective-permute-start | bytes 98312 | tf_op jit(solution)/shard_map/ppermute | solution.py:19
  23.4 5.8 %collective-permute-start.1 = (bf16[1,64,256]{2,1,0:T(8,128)(2,1)S(1)}, bf16[1,64,256]{2,1,0:T(8,128)(2,1)S(1)}, u32[]{:S(2)}, u32[]{:S(2)}) collective-permute-start(bf16[1,64,256]{2,1,0:T(8,128)(2,1)S(1)} %get-tuple-element.72), channel_id=1, source_target_pairs={{1,0},{2,1},{3,2},{5,4},{6,5},{7,6},{9,8},{10,9},{11,10},{13,12},{... | collective-permute-start | bytes 98312 | tf_op jit(solution)/shard_map/ppermute | solution.py:22
  24.7 70.9 %copy-start.31 = (pred[514]{0:T(1024)(128)(4,1)}, pred[514]{0:T(1024)(128)(4,1)S(1)}, u32[]{:S(2)}) copy-start(pred[514]{0:T(1024)(128)(4,1)S(1)} %broadcast_compare_fusion.1) | copy-start | bytes 1546
  24.8 70.4 %copy-start.33 = (pred[514]{0:T(1024)(128)(4,1)}, pred[514]{0:T(1024)(128)(4,1)S(1)}, u32[]{:S(2)}) copy-start(pred[514]{0:T(1024)(128)(4,1)S(1)} %broadcast_compare_fusion) | copy-start | bytes 1546
  30.1 23.9 %copy-start.11 = (f32[1,82944]{1,0:T(1,128)S(1)}, f32[1,82944]{1,0:T(1,128)}, u32[]{:S(2)}) copy-start(f32[1,82944]{1,0:T(1,128)} %param.8) | copy-start | bytes 995332
  53.1 0.9 copy-start.9
  87.9 7.5 %copy-start.20 = (bf16[4,64,256]{2,1,0:T(8,128)(2,1)}, bf16[4,64,256]{2,1,0:T(8,128)(2,1)S(1)}, u32[]{:S(2)}) copy-start(bf16[4,64,256]{2,1,0:T(8,128)(2,1)S(1)} %get-tuple-element.73) | copy-start | bytes 393220
  87.9 3.2 %collective-permute-start.2 = (bf16[1,64,256]{2,1,0:T(8,128)(2,1)S(1)}, bf16[1,64,256]{2,1,0:T(8,128)(2,1)S(1)}, u32[]{:S(2)}, u32[]{:S(2)}) collective-permute-start(bf16[1,64,256]{2,1,0:T(8,128)(2,1)S(1)} %get-tuple-element.69), channel_id=1, source_target_pairs={{0,1},{1,2},{2,3},{4,5},{5,6},{6,7},{8,9},{9,10},{10,11},{12,13},{... | collective-permute-start | bytes 98312 | tf_op jit(solution)/shard_map/ppermute | solution.py:19
  89.2 6.0 %collective-permute-start.3 = (bf16[1,64,256]{2,1,0:T(8,128)(2,1)S(1)}, bf16[1,64,256]{2,1,0:T(8,128)(2,1)S(1)}, u32[]{:S(2)}, u32[]{:S(2)}) collective-permute-start(bf16[1,64,256]{2,1,0:T(8,128)(2,1)S(1)} %get-tuple-element.70), channel_id=1, source_target_pairs={{1,0},{2,1},{3,2},{5,4},{6,5},{7,6},{9,8},{10,9},{11,10},{13,12},{... | collective-permute-start | bytes 98312 | tf_op jit(solution)/shard_map/ppermute | solution.py:22
  91.1 5.5 %copy-start.13 = (bf16[3,3,64,3,64]{2,4,3,1,0:T(8,128)(2,1)}, bf16[3,3,64,3,64]{2,4,3,1,0:T(8,128)(2,1)S(1)}, u32[]{:S(2)}) copy-start(bf16[3,3,64,3,64]{2,4,3,1,0:T(8,128)(2,1)S(1)} %copy.274) | copy-start | bytes 663556
  95.2 0.6 copy-start.28
  96.1 0.9 copy-start.21
  96.2 0.9 copy-start.29
  96.9 1.0 copy-start.14
  98.6 1.4 copy-start.1
  100.0 0.7 copy-start.18
  101.3 9.0 %collective-permute-start.4 = (bf16[1,64,256]{2,1,0:T(8,128)(2,1)}, bf16[1,64,256]{2,1,0:T(8,128)(2,1)S(1)}, u32[]{:S(2)}, u32[]{:S(2)}) collective-permute-start(bf16[1,64,256]{2,1,0:T(8,128)(2,1)} %get-tuple-element.67), channel_id=1, source_target_pairs={{0,1},{1,2},{2,3},{4,5},{5,6},{6,7},{8,9},{9,10},{10,11},{12,13},{... | collective-permute-start | bytes 98312 | tf_op jit(solution)/shard_map/ppermute | solution.py:19
  105.2 6.1 %collective-permute-start.5 = (bf16[1,64,256]{2,1,0:T(8,128)(2,1)}, bf16[1,64,256]{2,1,0:T(8,128)(2,1)}, u32[]{:S(2)}, u32[]{:S(2)}) collective-permute-start(bf16[1,64,256]{2,1,0:T(8,128)(2,1)} %get-tuple-element.68), channel_id=1, source_target_pairs={{1,0},{2,1},{3,2},{5,4},{6,5},{7,6},{9,8},{10,9},{11,10},{13,12},{... | collective-permute-start | bytes 98312 | tf_op jit(solution)/shard_map/ppermute | solution.py:22
  112.8 1.0 copy-start.15
  113.2 1.4 copy-start.3
  113.9 0.9 copy-start.19
  115.6 0.8 copy-start.5
  116.4 0.8 copy-start.7
  116.9 1.9 copy-start.35
  123.5 2.4 %copy-start.6 = (bf16[6,192,256]{2,1,0:T(8,128)(2,1)S(1)}, bf16[6,192,256]{2,1,0:T(8,128)(2,1)}, u32[]{:S(2)}) copy-start(bf16[6,192,256]{2,1,0:T(8,128)(2,1)} %copy-done.5) | copy-start | bytes 1769476
  123.5 2.7 %copy-start.4 = (bf16[6,192,256]{2,1,0:T(8,128)(2,1)S(1)}, bf16[6,192,256]{2,1,0:T(8,128)(2,1)}, u32[]{:S(2)}) copy-start(bf16[6,192,256]{2,1,0:T(8,128)(2,1)} %copy-done.3) | copy-start | bytes 1769476
  123.5 2.9 %copy-start.8 = (bf16[6,192,256]{2,1,0:T(8,128)(2,1)S(1)}, bf16[6,192,256]{2,1,0:T(8,128)(2,1)}, u32[]{:S(2)}) copy-start(bf16[6,192,256]{2,1,0:T(8,128)(2,1)} %copy-done.7) | copy-start | bytes 1769476
  124.7 3.3 %copy-start.16 = (bf16[4,64,256]{2,1,0:T(8,128)(2,1)}, bf16[4,64,256]{2,1,0:T(8,128)(2,1)S(1)}, u32[]{:S(2)}) copy-start(bf16[4,64,256]{2,1,0:T(8,128)(2,1)S(1)} %fusion.136) | copy-start | bytes 393220
  135.1 8.2 %collective-permute-start.6 = (bf16[1,64,256]{2,1,0:T(8,128)(2,1)}, bf16[1,64,256]{2,1,0:T(8,128)(2,1)S(1)}, u32[]{:S(2)}, u32[]{:S(2)}) collective-permute-start(bf16[1,64,256]{2,1,0:T(8,128)(2,1)} %get-tuple-element.65), channel_id=1, source_target_pairs={{0,1},{1,2},{2,3},{4,5},{5,6},{6,7},{8,9},{9,10},{10,11},{12,13},{... | collective-permute-start | bytes 98312 | tf_op jit(solution)/shard_map/ppermute | solution.py:19
  138.6 6.1 %collective-permute-start.7 = (bf16[1,64,256]{2,1,0:T(8,128)(2,1)}, bf16[1,64,256]{2,1,0:T(8,128)(2,1)}, u32[]{:S(2)}, u32[]{:S(2)}) collective-permute-start(bf16[1,64,256]{2,1,0:T(8,128)(2,1)} %get-tuple-element.66), channel_id=1, source_target_pairs={{1,0},{2,1},{3,2},{5,4},{6,5},{7,6},{9,8},{10,9},{11,10},{13,12},{... | collective-permute-start | bytes 98312 | tf_op jit(solution)/shard_map/ppermute | solution.py:22
  146.2 1.0 copy-start.23
  147.2 0.9 copy-start.17
  149.6 1.0 copy-start.27
  149.9 1.1 copy-start.2
  155.2 3.8 %copy-start.30 = (bf16[64,192]{1,0:T(8,128)(2,1)S(1)}, bf16[64,192]{1,0:T(8,128)(2,1)}, u32[]{:S(2)}) copy-start(bf16[64,192]{1,0:T(8,128)(2,1)} %fusion.16) | copy-start | bytes 73732
  159.7 5.3 %collective-permute-start.8 = (bf16[1,64,256]{2,1,0:T(8,128)(2,1)}, bf16[1,64,256]{2,1,0:T(8,128)(2,1)S(1)}, u32[]{:S(2)}, u32[]{:S(2)}) collective-permute-start(bf16[1,64,256]{2,1,0:T(8,128)(2,1)} %get-tuple-element.63), channel_id=1, source_target_pairs={{0,1},{1,2},{2,3},{4,5},{5,6},{6,7},{8,9},{9,10},{10,11},{12,13},{... | collective-permute-start | bytes 98312 | tf_op jit(solution)/shard_map/ppermute | solution.py:19
  162.8 6.0 %collective-permute-start.9 = (bf16[1,64,256]{2,1,0:T(8,128)(2,1)}, bf16[1,64,256]{2,1,0:T(8,128)(2,1)S(1)}, u32[]{:S(2)}, u32[]{:S(2)}) collective-permute-start(bf16[1,64,256]{2,1,0:T(8,128)(2,1)} %get-tuple-element.64), channel_id=1, source_target_pairs={{1,0},{2,1},{3,2},{5,4},{6,5},{7,6},{9,8},{10,9},{11,10},{13,12},{... | collective-permute-start | bytes 98312 | tf_op jit(solution)/shard_map/ppermute | solution.py:22
  164.3 4.5 %copy-start.32 = (pred[514]{0:T(1024)(128)(4,1)S(1)}, pred[514]{0:T(1024)(128)(4,1)}, u32[]{:S(2)}) copy-start(pred[514]{0:T(1024)(128)(4,1)} %copy-done.31) | copy-start | bytes 1546
  164.3 4.5 %copy-start.34 = (pred[514]{0:T(1024)(128)(4,1)S(1)}, pred[514]{0:T(1024)(128)(4,1)}, u32[]{:S(2)}) copy-start(pred[514]{0:T(1024)(128)(4,1)} %copy-done.33) | copy-start | bytes 1546
  169.4 1.0 copy-start.22
  171.9 1.0 copy-start.26
  177.1 43.6 %copy-start.10 = (f32[1,2,82944]{2,1,0:T(2,128)S(1)}, f32[1,2,82944]{2,1,0:T(2,128)}, u32[]{:S(2)}) copy-start(f32[1,2,82944]{2,1,0:T(2,128)} %copy-done.9) | copy-start | bytes 1990660
  177.1 43.6 %copy-start.12 = (f32[1,82944]{1,0:T(1,128)S(1)}, f32[1,82944]{1,0:T(1,128)}, u32[]{:S(2)}) copy-start(f32[1,82944]{1,0:T(1,128)} %param.8) | copy-start | bytes 995332
  177.1 43.6 %copy-start.24 = (f32[1,82944]{1,0:T(1,128)S(1)}, f32[1,82944]{1,0:T(1,128)}, u32[]{:S(2)}) copy-start(f32[1,82944]{1,0:T(1,128)} %param.9) | copy-start | bytes 995332
Sparse Core Ops, SparseCore 0:
  178.2 41.5 all-reduce.6
where the time goes:
time: 231 us; the launch traced here: 230 us
  waiting for transfers between devices  75.1 us (33%)
  local copies, waits for them, and re-layouts  39.8 us (17%)
  starting transfers between devices  28.2 us (12%)
  blocking collectives  25.9 us (11%)
  matrix products  23.3 us (10%)
  other arithmetic  19.5 us (8%)
  between operations  17.9 us (8%)
    psum x1, waiting for transfers between devices, on_device(): lax.psum(local_grad.astype(jnp.bfloat16), 'depth').astype(jnp.float32)  41.7 us
    all_gather x1, blocking collectives, on_device(): lax.all_gather(chosen_weight.astype(jnp.bfloat16), 'depth', axis=1, tiled...  25.9 us
    all_to_all x1, waiting for transfers between devices, on_device(): lax.all_to_all(outgoing.astype(jnp.bfloat16), 'trainer', split_axis=0, co...  21.7 us
    ppermute x5, starting transfers between devices, extended(): lax.ppermute(lax.slice_in_dim(block, block.shape[dim] - width, None, axis...  16 us
    ppermute x5, waiting for transfers between devices, extended(): lax.ppermute(lax.slice_in_dim(block, 0, width, axis=dim), axis, backward)  11.6 us
    dot_general x45, matrix products, convolve_grouped(): jnp.einsum('oj,zjs->zos', grouped[read_z, read_y], window[read_z:read_z +...  11.4 us
    another operation x27, local copies, waits for them, and re-layouts  10.8 us
    dot_general x27, matrix products, kernel_grad(): jnp.einsum('zos,zjs->oj', gradient, window[read_z:read_z + planes], prefe...  10.3 us
  transfers between devices with their start and end apart: 12, of which 7 were waited for; matrix products, arithmetic and copies ran while one was open for 4% of the time, Pallas kernels for 0%

commit v1 on v0

--- a/solution.py
+++ b/solution.py
@@ -1,6 +1,10 @@
+import functools
+
 import jax
 import jax.numpy as jnp
 from jax import lax
+from jax.experimental import pallas as pl
+from jax.experimental.pallas import tpu as pltpu
 from jax.sharding import PartitionSpec as P
 
 Y = 2
@@ -138,7 +142,7 @@
     return spread.reshape(planes, channels, cells)
 
 
-def on_device(noise, gen_weight, gen_momentum, disc_weight, score_weight, pairing, flags):
+def on_device_split(noise, gen_weight, gen_momentum, disc_weight, score_weight, pairing, flags):
     trainer_rank = lax.axis_index("trainer")
     partner = pairing[trainer_rank]
     keeper = flags[trainer_rank] == 1
@@ -187,6 +191,466 @@
     return (generated[None], new_weight, new_momentum)
 
 
+MESH = pl.DeviceIdType.MESH
+VMEM_LIMIT = 56 * 1024 * 1024
+WHOLE_PLANES = 16
+
+
+def bit_orders(count):
+    bits = [1 << k for k in range(count.bit_length() - 1)]
+    return bits[1:] + bits[:1], bits[:0:-1] + bits[:1]
+
+
+def flipped(index, bit):
+    return index + bit - 2 * bit * lax.rem(index // bit, 2)
+
+
+def doubling(slots, order, rank, send_sem, recv_sem):
+    for k, bit in enumerate(order):
+        copy = pltpu.make_async_remote_copy(
+            src_ref=slots.at[pl.ds(0, 1 << k)],
+            dst_ref=slots.at[pl.ds(1 << k, 1 << k)],
+            send_sem=send_sem.at[k],
+            recv_sem=recv_sem.at[k],
+            device_id={"trainer": flipped(rank, bit)},
+            device_id_type=MESH,
+        )
+        copy.start()
+        yield
+        copy.wait()
+
+
+def line_gather(slots, place, count, up_send, up_recv, down_send, down_recv):
+    def move(slot, target, send_sem, recv_sem):
+        return pltpu.make_async_remote_copy(
+            src_ref=slots.at[slot],
+            dst_ref=slots.at[slot],
+            send_sem=send_sem,
+            recv_sem=recv_sem,
+            device_id={"depth": target},
+            device_id_type=MESH,
+        )
+
+    def up(step):
+        return move(jnp.maximum(place - step, 0), place + 1, up_send.at[step], up_recv.at[step])
+
+    def down(step):
+        return move(
+            jnp.minimum(place + step, count - 1), place - 1, down_send.at[step], down_recv.at[step]
+        )
+
+    for step in range(count - 1):
+
+        @pl.when((place < count - 1) & (place >= step))
+        def _():
+            up(step).start()
+
+        @pl.when((place > 0) & (place + step <= count - 1))
+        def _():
+            down(step).start()
+
+        yield
+
+        @pl.when(place >= step + 1)
+        def _():
+            up(step).wait_recv()
+
+        @pl.when(place + step + 1 <= count - 1)
+        def _():
+            down(step).wait_recv()
+
+    for step in range(count - 1):
+
+        @pl.when((place < count - 1) & (place >= step))
+        def _():
+            up(step).wait_send()
+
+        @pl.when((place > 0) & (place + step <= count - 1))
+        def _():
+            down(step).wait_send()
+
+
+def advance(*steps):
+    alive = False
+    for each in steps:
+        alive = next(each, 0) is None or alive
+    return alive
+
+
+def exchange_kernel(
+    trainers,
+    depth,
+    pick_ref,
+    weight_ref,
+    moment_ref,
+    noise_ref,
+    kernels_ref,
+    volume_ref,
+    near_weight_ref,
+    near_moment_ref,
+    weight_a,
+    weight_b,
+    moment_a,
+    moment_b,
+    send_sem,
+    recv_sem,
+    line_sem,
+):
+    rank = lax.axis_index("trainer")
+    place = lax.axis_index("depth")
+    order_a, order_b = bit_orders(trainers)
+    barrier = pltpu.get_barrier_semaphore()
+    for bit in order_a:
+        pl.semaphore_signal(
+            barrier, inc=1, device_id={"trainer": flipped(rank, bit)}, device_id_type=MESH
+        )
+
+    @pl.when(place > 0)
+    def _():
+        pl.semaphore_signal(barrier, inc=1, device_id={"depth": place - 1}, device_id_type=MESH)
+
+    @pl.when(place < depth - 1)
+    def _():
+        pl.semaphore_signal(barrier, inc=1, device_id={"depth": place + 1}, device_id_type=MESH)
+
+    half = weight_a.shape[1]
+    padding = jnp.zeros((2 * half - weight_ref.shape[0], weight_ref.shape[1]), jnp.float32)
+    weight_a[0] = weight_ref[:half].astype(jnp.bfloat16)
+    weight_b[0] = jnp.concatenate([weight_ref[half:], padding], axis=0).astype(jnp.bfloat16)
+    moment_a[0] = moment_ref[:half].astype(jnp.bfloat16)
+    moment_b[0] = jnp.concatenate([moment_ref[half:], padding], axis=0).astype(jnp.bfloat16)
+    volume_ref[place] = noise_ref[...]
+
+    beside = (place > 0).astype(jnp.int32) + (place < depth - 1).astype(jnp.int32)
+    pl.semaphore_wait(barrier, len(order_a) + beside)
+
+    planes = line_gather(
+        volume_ref, place, depth, line_sem.at[0], line_sem.at[1], line_sem.at[2], line_sem.at[3]
+    )
+    first = doubling(weight_a, order_a, rank, send_sem.at[0], recv_sem.at[0])
+    second = doubling(weight_b, order_b, rank, send_sem.at[1], recv_sem.at[1])
+    advance(first, second, planes)
+    while advance(first, second):
+        advance(planes)
+
+    near_weight_ref[:half] = weight_a[pick_ref[0]]
+    near_weight_ref[half:] = weight_b[pick_ref[1]]
+    kernels_ref[place] = near_weight_ref[...]
+    share = line_gather(
+        kernels_ref, place, depth, line_sem.at[4], line_sem.at[5], line_sem.at[6], line_sem.at[7]
+    )
+    third = doubling(moment_a, order_a, rank, send_sem.at[2], recv_sem.at[2])
+    fourth = doubling(moment_b, order_b, rank, send_sem.at[3], recv_sem.at[3])
+    advance(share, third, fourth)
+    while advance(planes):
+        pass
+    while advance(share, third, fourth):
+        pass
+    near_moment_ref[:half] = moment_a[pick_ref[0]]
+    near_moment_ref[half:] = moment_b[pick_ref[1]]
+
+
+def exchange(trainers, depth, picks, weight, moment, noise):
+    rows = weight.shape[0]
+    half = -(-rows // 32) * 16
+    levels = trainers.bit_length() - 1
+    vmem = pl.BlockSpec(memory_space=pltpu.VMEM)
+    slots = pltpu.VMEM((trainers, half, X), jnp.bfloat16)
+    near = jax.ShapeDtypeStruct((2 * half, X), jnp.bfloat16)
+    return pl.pallas_call(
+        functools.partial(exchange_kernel, trainers, depth),
+        out_shape=(
+            jax.ShapeDtypeStruct((depth, 2 * half, X), jnp.bfloat16),
+            jax.ShapeDtypeStruct((depth,) + noise.shape, jnp.bfloat16),
+            near,
+            near,
+        ),
+        in_specs=[pl.BlockSpec(memory_space=pltpu.SMEM), vmem, vmem, vmem],
+        out_specs=(vmem,) * 4,
+        scratch_shapes=[
+            slots,
+            slots,
+            slots,
+            slots,
+            pltpu.SemaphoreType.DMA((4, levels)),
+            pltpu.SemaphoreType.DMA((4, levels)),
+            pltpu.SemaphoreType.DMA((8, depth - 1)),
+        ],
+        compiler_params=pltpu.CompilerParams(
+            collective_id=0, has_side_effects=True, vmem_limit_bytes=VMEM_LIMIT
+        ),
+    )(picks, weight, moment, noise)
+
+
+ROOT = 0.7978845608028654
+CUBIC = 0.044715
+
+
+def gelu_of(inputs):
+    bend = jnp.tanh(ROOT * (inputs + CUBIC * (inputs * inputs * inputs)))
+    return 0.5 * inputs * (1.0 + bend)
+
+
+def gelu_slope(inputs):
+    square = inputs * inputs
+    bend = jnp.tanh(ROOT * (inputs + CUBIC * (square * inputs)))
+    tilt = ROOT * (1.0 + 3.0 * CUBIC * square)
+    return 0.5 * (1.0 + bend) + 0.5 * inputs * (1.0 - bend * bend) * tilt
+
+
+def dot(left, right):
+    return jnp.dot(left, right, preferred_element_type=jnp.float32)
+
+
+def dot_rows(left, right):
+    return lax.dot_general(
+        left, right, (((1,), (1,)), ((), ())), preferred_element_type=jnp.float32
+    )
+
+
+def trainer_kernel(
+    planes,
+    pick_ref,
+    kernels_ref,
+    noise_ref,
+    disc_ref,
+    score_ref,
+    weight_ref,
+    moment_ref,
+    near_weight_ref,
+    near_moment_ref,
+    made_ref,
+    new_weight_ref,
+    new_moment_ref,
+    square_ref,
+    fore_ref,
+    back_ref,
+    inputs_ref,
+    grads_ref,
+    pre_ref,
+    made_all,
+):
+    channels = noise_ref.shape[1]
+    wide = 2 * channels
+    cells = planes * X
+    shares, share_rows = kernels_ref.shape[0], weight_ref.shape[0]
+    lane = lax.broadcasted_iota(jnp.int32, (wide, X), 1)
+
+    def put(buffer, plane, value):
+        columns = pl.ds(pl.multiple_of((plane + 1) * X, X), X)
+        low = jnp.where(lane == 0, 0.0, pltpu.roll(value, 1, 1))
+        high = jnp.where(lane == X - 1, 0.0, pltpu.roll(value, X - 1, 1))
+        buffer[0:wide, columns] = low.astype(jnp.bfloat16)
+        buffer[wide : 2 * wide, columns] = value.astype(jnp.bfloat16)
+        buffer[2 * wide : 3 * wide, columns] = high.astype(jnp.bfloat16)
+
+    empty = jnp.zeros((3 * wide, X), jnp.bfloat16)
+    for buffer in [inputs_ref.at[k] for k in range(3)] + [grads_ref.at[k] for k in range(2)]:
+        buffer[:, 0:X] = empty
+        buffer[:, cells + X : cells + 2 * X] = empty
+
+    for part in range(shares):
+        rows = kernels_ref[part].astype(jnp.float32)[:share_rows]
+        begin = 2 * part * share_rows
+        square_ref[pl.ds(begin, share_rows, stride=2), :] = rows[:, :channels]
+        square_ref[pl.ds(begin + 1, share_rows, stride=2), :] = rows[:, channels:]
+
+    def tap(layer, a, b, c):
+        begin = (27 * layer + 9 * a + 3 * b + c) * channels
+        return square_ref[begin : begin + channels, :]
+
+    for layer in range(3):
+        for a in range(3):
+            for c in range(3):
+                middle = tap(layer, a, 1, c)
+                block = jnp.concatenate(
+                    [
+                        jnp.concatenate([middle, tap(layer, a, 2, c)], axis=1),
+                        jnp.concatenate([tap(layer, a, 0, c), middle], axis=1),
+                    ],
+                    axis=0,
+                )
+                fore_ref[layer, a, :, c * wide : (c + 1) * wide] = block.astype(jnp.bfloat16)
+                if layer:
+                    back_ref[layer - 1, 2 - a, :, (2 - c) * wide : (3 - c) * wide] = (
+                        block.T.astype(jnp.bfloat16)
+                    )
+
+    def convolved(weights, buffer, pair):
+        total = None
+        for a in range(3):
+            columns = pl.ds(pl.multiple_of((2 * pair + a) * X, X), 2 * X)
+            term = dot(weights[a], buffer[:, columns])
+            total = term if total is None else total + term
+        return total
+
+    @pl.loop(0, planes)
+    def _(plane):
+        both = noise_ref[plane].astype(jnp.float32)
+        put(inputs_ref.at[0], plane, jnp.concatenate([both[:, :X], both[:, X:]], axis=0))
+
+    for layer in range(2):
+
+        @pl.loop(0, planes // 2)
+        def _(pair):
+            total = convolved(fore_ref.at[layer], inputs_ref.at[layer], pair)
+            pre_ref[layer, :, pl.ds(pl.multiple_of(2 * pair * X, X), 2 * X)] = total
+            act = gelu_of(total)
+            put(inputs_ref.at[layer + 1], 2 * pair, act[:, :X])
+            put(inputs_ref.at[layer + 1], 2 * pair + 1, act[:, X:])
+
+    critic = jnp.concatenate([disc_ref[4 * a + 2 * b + d] for a in range(2) for d in range(2) for b in range(2)], axis=1)
+    critic_back = jnp.concatenate(
+        [
+            jnp.concatenate(
+                [
+                    critic[:, (2 * a + d) * wide : (2 * a + d + 1) * wide].astype(jnp.float32).T
+                    for d in range(2)
+                ],
+                axis=1,
+            )
+            for a in range(2)
+        ],
+        axis=0,
+    ).astype(jnp.bfloat16)
+    features = disc_ref.shape[1]
+    score = jnp.broadcast_to(score_ref[...], (X, features)).T
+
+    @pl.loop(0, planes // 2)
+    def _(pair):
+        made = jnp.tanh(convolved(fore_ref.at[2], inputs_ref.at[2], pair))
+        rounded = made.astype(jnp.bfloat16)
+        exact = rounded.astype(jnp.float32)
+        for a in range(2):
+            plane = rounded[:, a * X : (a + 1) * X]
+            made_all[2 * pair + a, :, 0:X] = plane[:channels]
+            made_all[2 * pair + a, :, X : 2 * X] = plane[channels:]
+        pieces = []
+        for a in range(2):
+            plane = exact[:, a * X : (a + 1) * X]
+            pieces += [plane, pltpu.roll(plane, X - 1, 1)]
+        response = dot(critic, jnp.concatenate(pieces, axis=0).astype(jnp.bfloat16))
+        scores = jnp.sum(score * gelu_of(response), axis=0, keepdims=True)
+        slope = -jax.nn.sigmoid(-scores)
+        upstream = gelu_slope(response) * (slope * score)
+        upstream = jnp.where(lax.rem(lane, 2) == 0, upstream, 0.0)
+        pieces = jnp.concatenate([upstream, pltpu.roll(upstream, 1, 1)], axis=0)
+        spread = dot(critic_back, pieces.astype(jnp.bfloat16))
+        for a in range(2):
+            plane = made[:, a * X : (a + 1) * X]
+            put(grads_ref.at[0], 2 * pair + a, spread[a * wide : (a + 1) * wide] * (1.0 - plane * plane))
+
+    def kernel_sums(layer, gradient):
+        for a in range(3):
+            sums = dot_rows(gradient, inputs_ref[layer, :, a * X : a * X + cells])
+            for c in range(3):
+                block = sums[:, c * wide : (c + 1) * wide]
+                parts = (
+                    block[channels:, :channels],
+                    block[:channels, :channels] + block[channels:, channels:],
+                    block[:channels, channels:],
+                )
+                for b in range(3):
+                    begin = (27 * layer + 9 * a + 3 * b + c) * channels
+                    square_ref[begin : begin + channels, :] = parts[b]
+
+    for layer in (2, 1):
+        held = grads_ref.at[2 - layer]
+        kernel_sums(layer, held[wide : 2 * wide, X : X + cells])
+
+        @pl.loop(0, planes // 2)
+        def _(pair):
+            columns = pl.ds(pl.multiple_of(2 * pair * X, X), 2 * X)
+            total = convolved(back_ref.at[layer - 1], held, pair)
+            total = total * gelu_slope(pre_ref[layer - 1, :, columns])
+            if layer == 2:
+                put(grads_ref.at[1], 2 * pair, total[:, :X])
+                put(grads_ref.at[1], 2 * pair + 1, total[:, X:])
+            else:
+                later = pl.ds(pl.multiple_of((2 * pair + 1) * X, X), 2 * X)
+                grads_ref[0, wide : 2 * wide, later] = total.astype(jnp.bfloat16)
+
+    kernel_sums(0, grads_ref[0, wide : 2 * wide, X : X + cells])
+
+    keep = pick_ref[2] == 1
+    place = pick_ref[3]
+    own_planes = made_ref.shape[0]
+    made_ref[...] = made_all[pl.ds(place * own_planes, own_planes)]
+    begin = 2 * place * share_rows
+    sums = jnp.concatenate(
+        [
+            square_ref[pl.ds(begin, share_rows, stride=2), :],
+            square_ref[pl.ds(begin + 1, share_rows, stride=2), :],
+        ],
+        axis=1,
+    )
+    near_moment = near_moment_ref[...].astype(jnp.float32)[:share_rows]
+    near_weight = near_weight_ref[...].astype(jnp.float32)[:share_rows]
+    moment = momentum_decay * jnp.where(keep, moment_ref[...], near_moment) + sums
+    new_moment_ref[...] = moment
+    new_weight_ref[...] = jnp.where(keep, weight_ref[...], near_weight) - step_length * moment
+
+
+def train(picks, kernels, volume, disc, score, weight, moment, near_weight, near_moment, own):
+    planes, channels = volume.shape[0], volume.shape[1]
+    wide = 2 * channels
+    framed = (planes + 2) * X
+    vmem = pl.BlockSpec(memory_space=pltpu.VMEM)
+    return pl.pallas_call(
+        functools.partial(trainer_kernel, planes),
+        out_shape=(
+            jax.ShapeDtypeStruct((own,) + volume.shape[1:], jnp.bfloat16),
+            jax.ShapeDtypeStruct(weight.shape, jnp.float32),
+            jax.ShapeDtypeStruct(weight.shape, jnp.float32),
+        ),
+        in_specs=[pl.BlockSpec(memory_space=pltpu.SMEM)] + [vmem] * 8,
+        out_specs=(vmem,) * 3,
+        scratch_shapes=[
+            pltpu.VMEM((81 * channels, channels), jnp.float32),
+            pltpu.VMEM((3, 3, wide, 3 * wide), jnp.bfloat16),
+            pltpu.VMEM((2, 3, wide, 3 * wide), jnp.bfloat16),
+            pltpu.VMEM((3, 3 * wide, framed), jnp.bfloat16),
+            pltpu.VMEM((2, 3 * wide, framed), jnp.bfloat16),
+            pltpu.VMEM((2, wide, planes * X), jnp.float32),
+            pltpu.VMEM(volume.shape, jnp.bfloat16),
+        ],
+        compiler_params=pltpu.CompilerParams(vmem_limit_bytes=VMEM_LIMIT),
+    )(picks, kernels, volume, disc, score, weight, moment, near_weight, near_moment)
+
+
+def on_device(trainers, depth, noise, gen_weight, gen_momentum, disc_weight, score_weight, pairing, flags):
+    own = noise.shape[1]
+    if own * depth > WHOLE_PLANES or depth < 2 or trainers & (trainers - 1):
+        return on_device_split(
+            noise, gen_weight, gen_momentum, disc_weight, score_weight, pairing, flags
+        )
+    rank = lax.axis_index("trainer")
+    place = lax.axis_index("depth")
+    partner, keeper = pairing[rank], flags[rank]
+    apart = jnp.where(keeper == 1, 0, jnp.bitwise_xor(rank, partner))
+    picks = []
+    for order in bit_orders(trainers):
+        picks.append(sum(((apart // bit) % 2) << k for k, bit in enumerate(order)))
+    picks = jnp.stack(picks + [keeper, place]).astype(jnp.int32)
+    weight, moment = gen_weight.reshape(-1, X), gen_momentum.reshape(-1, X)
+    kernels, volume, near_weight, near_moment = exchange(
+        trainers, depth, picks, weight, moment, noise[0]
+    )
+    made, new_weight, new_moment = train(
+        picks,
+        kernels,
+        volume.reshape((own * depth,) + noise.shape[2:]),
+        disc_weight[0],
+        score_weight,
+        weight,
+        moment,
+        near_weight,
+        near_moment,
+        own,
+    )
+    return made[None], new_weight.reshape(gen_weight.shape), new_moment.reshape(gen_weight.shape)
+
+
 def solution(mesh):
     placed = (
         P("trainer", "depth", None, None),
@@ -198,7 +662,7 @@
         P(),
     )
     return jax.shard_map(
-        on_device,
+        functools.partial(on_device, mesh.shape["trainer"], mesh.shape["depth"]),
         mesh=mesh,
         in_specs=placed,
         out_specs=(P("trainer", "depth", None, None), P("trainer", "depth"), P("trainer", "depth")),

time: 231 us -> 69.6 us (0.30)
  waiting for transfers between devices: 75.1 us -> 0 us
  Pallas kernels: 0 us -> 62.6 us
  local copies, waits for them, and re-layouts: 39.8 us -> 3.45 us
  starting transfers between devices: 28.2 us -> 0 us
  blocking collectives: 25.9 us -> 0 us
  matrix products: 23.3 us -> 0 us
  other arithmetic: 19.5 us -> 1.29 us
  between operations: 17.9 us -> 2.02 us
    pallas_call x0 -> x2, Pallas kernels: none -> 62.6 us  [the longest x1 34 us: exchange(): pl.pallas_call(functools.partial(exchange_kernel, trainers, depth), out_s...]
    psum x1 -> x0, waiting for transfers between devices: 41.7 us -> none  [on_device(): lax.psum(local_grad.astype(jnp.bfloat16), 'depth').astype(jnp.float32)]
    all_gather x1 -> x0, blocking collectives: 25.9 us -> none  [on_device(): lax.all_gather(chosen_weight.astype(jnp.bfloat16), 'depth', axis=1, tiled...]
    dot_general x74 -> x0, matrix products: 23.3 us -> none  [the longest x45 11.4 us: convolve_grouped(): jnp.einsum('oj,zjs->zos', grouped[read_z, read_y], window[read_z:read_z +...]
    ppermute x10 -> x0, starting transfers between devices: 22.8 us -> none  [the longest x5 16 us: extended(): lax.ppermute(lax.slice_in_dim(block, block.shape[dim] - width, None, axis...]
    all_to_all x1 -> x0, waiting for transfers between devices: 21.7 us -> none  [on_device(): lax.all_to_all(outgoing.astype(jnp.bfloat16), 'trainer', split_axis=0, co...]
    another operation x34 -> x0, local copies, waits for them, and re-layouts: 14.3 us -> none
    ppermute x10 -> x0, waiting for transfers between devices: 11.6 us -> none  [the longest x5 11.6 us: extended(): lax.ppermute(lax.slice_in_dim(block, 0, width, axis=dim), axis, backward)]
  transfers between devices with their start and end apart: 12 -> 0, of which waited for: 7 -> 0; matrix products, arithmetic and copies ran while one was open for 4% -> 0% of each run, Pallas kernels for 0% -> 0%
where the time goes in v1:
time: 69.6 us; the launch traced here: 69.4 us
  Pallas kernels  62.6 us (90%)
  local copies, waits for them, and re-layouts  3.45 us (5%)
  between operations  2.02 us (3%)
  other arithmetic  1.29 us (2%)
    pallas_call x1, Pallas kernels, exchange(): pl.pallas_call(functools.partial(exchange_kernel, trainers, depth), out_s...  34 us
    pallas_call x1, Pallas kernels, train(): pl.pallas_call(functools.partial(trainer_kernel, planes), out_shape=(jax....  28.7 us
    dynamic_slice x2, local copies, waits for them, and re-layouts, on_device(): partner, keeper = (pairing[rank], flags[rank])  2.58 us

profile of v1, /device:TPU:0, one launch (start us, length us, event | category | flops | bytes accessed | tf_op | source)
XLA Modules:
  0.0 69.4 jit_solution(14105210644367166090)
XLA Ops:
  0.6 0.0 copy-start
  0.6 1.3 %dynamic_slice.6 = s32[1]{0:T(128)} dynamic-slice(s32[8]{0:T(128)} %param.13, s32[]{:T(128)S(6)} %select_n.40), dynamic_slice_sizes={1} | dynamic-slice | bytes 12 | tf_op jit(solution)/shard_map/dynamic_slice | solution.py:629
  2.6 1.3 %dynamic_slice.7 = s32[1]{0:T(128)} dynamic-slice(s32[8]{0:T(128)} %param.12, s32[]{:T(128)S(6)} %select_n.40), dynamic_slice_sizes={1} | dynamic-slice | bytes 12 | tf_op jit(solution)/shard_map/dynamic_slice | solution.py:629
  4.6 1.3 %pad_add_fusion.pick_ref = s32[4]{0:T(128)} fusion(s32[1]{0:T(128)} %bitcast.4, s32[1]{0:T(128)} %dynamic_slice.6, s32[1]{0:T(128)} %bitcast.3, s32[1]{0:T(128)} %bitcast.2), kind=kLoop, calls=%fused_computation | loop fusion | flops 12 | bytes 32 | tf_op jit(solution)/shard_map/stack | solution.py:634
  5.9 0.0 copy-done
  5.9 0.9 %copy.10 = bf16[1,8,128,64]{3,2,1,0:T(8,128)(2,1)} copy(bf16[1,8,128,64]{2,3,1,0:T(8,128)(2,1)S(1)} %copy-done) | data formatting | bytes 262144 | tf_op args[3]
  6.8 34.0 %shard_map.94 = (bf16[4,672,128]{2,1,0:T(8,128)(2,1)}, bf16[4,4,64,256]{3,2,1,0:T(8,128)(2,1)}, bf16[672,128]{1,0:T(8,128)(2,1)}, bf16[672,128]{1,0:T(8,128)(2,1)}) custom-call(s32[4]{0:T(128)} %pad_add_fusion.pick_ref, f32[648,128]{1,0:T(8,128)} %bitcast.13, f32[648,128]{1,0:T(8,128)} %bitcast.15, bf16[4,64,256]{2,1,0:T(8,128)(2,1)} %bitcast.19), custom_call_target="tpu_custom_call" | custom-call | tf_op jit(solution)/shard_map/pallas_call | solution.py:360
  40.7 28.7 %shard_map.95 = (bf16[4,64,256]{2,1,0:T(8,128)(2,1)}, f32[648,128]{1,0:T(8,128)}, f32[648,128]{1,0:T(8,128)}) custom-call(s32[4]{0:T(128)} %pad_add_fusion.pick_ref, bf16[4,672,128]{2,1,0:T(8,128)(2,1)} %get-tuple-element.10.kernels_ref, bf16[16,64,256]{2,1,0:T(8,128)(2,1)} %bitcast.18, bf16[8,128,64]{2,1,0:T(8,128)(2,1)} %bitcast.17, f32[1,128]{1,0:T(1,128)} %score_ref.1, ...), custom_call_target="tpu_custom_call" | custom-call | tf_op jit(solution)/shard_map/pallas_call | solution.py:599
Async XLA Ops:
  0.6 5.3 %copy-start = (bf16[1,8,128,64]{2,3,1,0:T(8,128)(2,1)S(1)}, bf16[1,8,128,64]{2,3,1,0:T(8,128)(2,1)}, u32[]{:S(2)}) copy-start(bf16[1,8,128,64]{2,3,1,0:T(8,128)(2,1)} %param.10) | copy-start | bytes 393220

commit v2 on v0

--- a/solution.py
+++ b/solution.py
@@ -1,6 +1,10 @@
+import functools
+
 import jax
 import jax.numpy as jnp
 from jax import lax
+from jax.experimental import pallas as pl
+from jax.experimental.pallas import tpu as pltpu
 from jax.sharding import PartitionSpec as P
 
 Y = 2
@@ -138,7 +142,7 @@
     return spread.reshape(planes, channels, cells)
 
 
-def on_device(noise, gen_weight, gen_momentum, disc_weight, score_weight, pairing, flags):
+def on_device_split(noise, gen_weight, gen_momentum, disc_weight, score_weight, pairing, flags):
     trainer_rank = lax.axis_index("trainer")
     partner = pairing[trainer_rank]
     keeper = flags[trainer_rank] == 1
@@ -187,6 +191,474 @@
     return (generated[None], new_weight, new_momentum)
 
 
+MESH = pl.DeviceIdType.MESH
+VMEM_LIMIT = 56 * 1024 * 1024
+WHOLE_PLANES = 16
+
+
+def bit_orders(count):
+    bits = [1 << k for k in range(count.bit_length() - 1)]
+    return bits[1:] + bits[:1], bits[:0:-1] + bits[:1]
+
+
+def flipped(index, bit):
+    return index + bit - 2 * bit * lax.rem(index // bit, 2)
+
+
+def doubling(slots, order, rank, send_sem, recv_sem):
+    for k, bit in enumerate(order):
+        copy = pltpu.make_async_remote_copy(
+            src_ref=slots.at[pl.ds(0, 1 << k)],
+            dst_ref=slots.at[pl.ds(1 << k, 1 << k)],
+            send_sem=send_sem.at[k],
+            recv_sem=recv_sem.at[k],
+            device_id={"trainer": flipped(rank, bit)},
+            device_id_type=MESH,
+        )
+        copy.start()
+        yield
+        copy.wait()
+
+
+def line_gather(slots, place, count, up_send, up_recv, down_send, down_recv):
+    def move(slot, target, send_sem, recv_sem):
+        return pltpu.make_async_remote_copy(
+            src_ref=slots.at[slot],
+            dst_ref=slots.at[slot],
+            send_sem=send_sem,
+            recv_sem=recv_sem,
+            device_id={"depth": target},
+            device_id_type=MESH,
+        )
+
+    def up(step):
+        return move(jnp.maximum(place - step, 0), place + 1, up_send.at[step], up_recv.at[step])
+
+    def down(step):
+        return move(
+            jnp.minimum(place + step, count - 1), place - 1, down_send.at[step], down_recv.at[step]
+        )
+
+    for step in range(count - 1):
+
+        @pl.when((place < count - 1) & (place >= step))
+        def _():
+            up(step).start()
+
+        @pl.when((place > 0) & (place + step <= count - 1))
+        def _():
+            down(step).start()
+
+        yield
+
+        @pl.when(place >= step + 1)
+        def _():
+            up(step).wait_recv()
+
+        @pl.when(place + step + 1 <= count - 1)
+        def _():
+            down(step).wait_recv()
+
+    yield
+    for step in range(count - 1):
+
+        @pl.when((place < count - 1) & (place >= step))
+        def _():
+            up(step).wait_send()
+
+        @pl.when((place > 0) & (place + step <= count - 1))
+        def _():
+            down(step).wait_send()
+
+
+def advance(*steps):
+    alive = False
+    for each in steps:
+        alive = next(each, 0) is None or alive
+    return alive
+
+
+ROOT = 0.7978845608028654
+CUBIC = 0.044715
+
+
+def gelu_of(inputs):
+    bend = jnp.tanh(ROOT * (inputs + CUBIC * (inputs * inputs * inputs)))
+    return 0.5 * inputs * (1.0 + bend)
+
+
+def gelu_slope(inputs):
+    square = inputs * inputs
+    bend = jnp.tanh(ROOT * (inputs + CUBIC * (square * inputs)))
+    tilt = ROOT * (1.0 + 3.0 * CUBIC * square)
+    return 0.5 * (1.0 + bend) + 0.5 * inputs * (1.0 - bend * bend) * tilt
+
+
+def dot(left, right):
+    return jnp.dot(left, right, preferred_element_type=jnp.float32)
+
+
+def dot_rows(left, right):
+    return lax.dot_general(
+        left, right, (((1,), (1,)), ((), ())), preferred_element_type=jnp.float32
+    )
+
+
+def round_kernel(
+    trainers,
+    depth,
+    pairing_ref,
+    flags_ref,
+    weight_ref,
+    moment_ref,
+    noise_ref,
+    disc_ref,
+    score_ref,
+    made_ref,
+    new_weight_ref,
+    new_moment_ref,
+    kernels_ref,
+    volume_ref,
+    weight_a,
+    weight_b,
+    moment_a,
+    moment_b,
+    square_ref,
+    fore_ref,
+    back_ref,
+    inputs_ref,
+    grads_ref,
+    pre_ref,
+    made_all,
+    critic_ref,
+    critic_back_ref,
+    send_sem,
+    recv_sem,
+    line_sem,
+):
+    own, channels = noise_ref.shape[0], noise_ref.shape[1]
+    planes = own * depth
+    wide = 2 * channels
+    cells = planes * X
+    share_rows = weight_ref.shape[0]
+    rank = lax.axis_index("trainer")
+    place = lax.axis_index("depth")
+    order_a, order_b = bit_orders(trainers)
+    barrier = pltpu.get_barrier_semaphore()
+    for bit in order_a:
+        pl.semaphore_signal(
+            barrier, inc=1, device_id={"trainer": flipped(rank, bit)}, device_id_type=MESH
+        )
+
+    @pl.when(place > 0)
+    def _():
+        pl.semaphore_signal(barrier, inc=1, device_id={"depth": place - 1}, device_id_type=MESH)
+
+    @pl.when(place < depth - 1)
+    def _():
+        pl.semaphore_signal(barrier, inc=1, device_id={"depth": place + 1}, device_id_type=MESH)
+
+    half = weight_a.shape[1]
+    padding = jnp.zeros((2 * half - share_rows, weight_ref.shape[1]), jnp.float32)
+    weight_a[0] = weight_ref[:half].astype(jnp.bfloat16)
+    weight_b[0] = jnp.concatenate([weight_ref[half:], padding], axis=0).astype(jnp.bfloat16)
+    moment_a[0] = moment_ref[:half].astype(jnp.bfloat16)
+    moment_b[0] = jnp.concatenate([moment_ref[half:], padding], axis=0).astype(jnp.bfloat16)
+    volume_ref[place] = noise_ref[...]
+
+    beside = (place > 0).astype(jnp.int32) + (place < depth - 1).astype(jnp.int32)
+    pl.semaphore_wait(barrier, len(order_a) + beside)
+
+    noise_line = line_gather(
+        volume_ref, place, depth, line_sem.at[0], line_sem.at[1], line_sem.at[2], line_sem.at[3]
+    )
+    first = doubling(weight_a, order_a, rank, send_sem.at[0], recv_sem.at[0])
+    second = doubling(weight_b, order_b, rank, send_sem.at[1], recv_sem.at[1])
+    third = doubling(moment_a, order_a, rank, send_sem.at[2], recv_sem.at[2])
+    fourth = doubling(moment_b, order_b, rank, send_sem.at[3], recv_sem.at[3])
+    share_line = line_gather(
+        kernels_ref, place, depth, line_sem.at[4], line_sem.at[5], line_sem.at[6], line_sem.at[7]
+    )
+    advance(first, second, noise_line)
+
+    lane = lax.broadcasted_iota(jnp.int32, (wide, X), 1)
+    blocks = [
+        [jnp.concatenate([disc_ref[4 * a + 2 * b + d] for b in range(2)], axis=0) for d in range(2)]
+        for a in range(2)
+    ]
+    for a in range(2):
+        for d in range(2):
+            at = 2 * a + d
+            critic_back_ref[a * wide : (a + 1) * wide, d * X : (d + 1) * X] = blocks[a][d]
+            critic_ref[:, at * wide : (at + 1) * wide] = (
+                blocks[a][d].astype(jnp.float32).T.astype(jnp.bfloat16)
+            )
+    empty = jnp.zeros((3 * wide, X), jnp.bfloat16)
+    for buffer in [inputs_ref.at[k] for k in range(3)] + [grads_ref.at[k] for k in range(2)]:
+        buffer[:, 0:X] = empty
+        buffer[:, cells + X : cells + 2 * X] = empty
+
+    while advance(first, second):
+        advance(noise_line)
+
+    keep = flags_ref[rank] == 1
+    partner = pairing_ref[rank]
+    picks = []
+    for order in (order_a, order_b):
+        pick = 0
+        for k, bit in enumerate(order):
+            differs = lax.rem(rank // bit + partner // bit, 2)
+            pick = pick + differs * (1 << k)
+        picks.append(jnp.where(keep, 0, pick))
+    kernels_ref[place, :half] = weight_a[picks[0]]
+    kernels_ref[place, half:] = weight_b[picks[1]]
+    advance(share_line, third, fourth)
+
+    def put(buffer, plane, value):
+        columns = pl.ds(pl.multiple_of((plane + 1) * X, X), X)
+        low = jnp.where(lane == 0, 0.0, pltpu.roll(value, 1, 1))
+        high = jnp.where(lane == X - 1, 0.0, pltpu.roll(value, X - 1, 1))
+        buffer[0:wide, columns] = low.astype(jnp.bfloat16)
+        buffer[wide : 2 * wide, columns] = value.astype(jnp.bfloat16)
+        buffer[2 * wide : 3 * wide, columns] = high.astype(jnp.bfloat16)
+
+    def unpack(part):
+        rows = kernels_ref[part].astype(jnp.float32)[:share_rows]
+        begin = pl.multiple_of(2 * part * share_rows, 8)
+        square_ref[pl.ds(begin, share_rows, stride=2), :] = rows[:, :channels]
+        square_ref[pl.ds(begin + 1, share_rows, stride=2), :] = rows[:, channels:]
+
+    def tap(layer, a, b, c):
+        begin = (27 * layer + 9 * a + 3 * b + c) * channels
+        return square_ref[begin : begin + channels, :]
+
+    def prepare(layer):
+        for a in range(3):
+            for c in range(3):
+                middle = tap(layer, a, 1, c)
+                block = jnp.concatenate(
+                    [
+                        jnp.concatenate([middle, tap(layer, a, 2, c)], axis=1),
+                        jnp.concatenate([tap(layer, a, 0, c), middle], axis=1),
+                    ],
+                    axis=0,
+                )
+                fore_ref[layer, a, :, c * wide : (c + 1) * wide] = block.astype(jnp.bfloat16)
+                if layer:
+                    back_ref[layer - 1, 2 - a, :, (2 - c) * wide : (3 - c) * wide] = (
+                        block.T.astype(jnp.bfloat16)
+                    )
+
+    def convolved(weights, buffer, pair):
+        total = None
+        for a in range(3):
+            columns = pl.ds(pl.multiple_of((2 * pair + a) * X, X), 2 * X)
+            term = dot(weights[a], buffer[:, columns])
+            total = term if total is None else total + term
+        return total
+
+    def forward(layer):
+        prepare(layer)
+
+        @pl.loop(0, planes // 2)
+        def _(pair):
+            total = convolved(fore_ref.at[layer], inputs_ref.at[layer], pair)
+            if layer < 2:
+                pre_ref[layer, :, pl.ds(pl.multiple_of(2 * pair * X, X), 2 * X)] = total
+                act = gelu_of(total)
+                put(inputs_ref.at[layer + 1], 2 * pair, act[:, :X])
+                put(inputs_ref.at[layer + 1], 2 * pair + 1, act[:, X:])
+            else:
+                criticise(pair, jnp.tanh(total))
+
+    score = jnp.broadcast_to(score_ref[...], (X, X)).T
+
+    def criticise(pair, made):
+        rounded = made.astype(jnp.bfloat16)
+        exact = rounded.astype(jnp.float32)
+        for a in range(2):
+            plane = rounded[:, a * X : (a + 1) * X]
+            made_all[2 * pair + a, :, 0:X] = plane[:channels]
+            made_all[2 * pair + a, :, X : 2 * X] = plane[channels:]
+        pieces = []
+        for a in range(2):
+            plane = exact[:, a * X : (a + 1) * X]
+            pieces += [plane, pltpu.roll(plane, X - 1, 1)]
+        response = dot(critic_ref[...], jnp.concatenate(pieces, axis=0).astype(jnp.bfloat16))
+        scores = jnp.sum(score * gelu_of(response), axis=0, keepdims=True)
+        slope = -jax.nn.sigmoid(-scores)
+        upstream = gelu_slope(response) * (slope * score)
+        upstream = jnp.where(lax.rem(lane, 2) == 0, upstream, 0.0)
+        pieces = jnp.concatenate([upstream, pltpu.roll(upstream, 1, 1)], axis=0)
+        spread = dot(critic_back_ref[...], pieces.astype(jnp.bfloat16))
+        for a in range(2):
+            plane = made[:, a * X : (a + 1) * X]
+            fall = 1.0 - plane * plane
+            put(grads_ref.at[0], 2 * pair + a, spread[a * wide : (a + 1) * wide] * fall)
+
+    unpack(place)
+    while advance(noise_line):
+        pass
+    for part in range(depth):
+
+        @pl.loop(0, own)
+        def _(plane):
+            both = volume_ref[part, plane].astype(jnp.float32)
+            whole = jnp.concatenate([both[:, :X], both[:, X:]], axis=0)
+            put(inputs_ref.at[0], part * own + plane, whole)
+
+    layer_rows = 27 * channels
+    edges = []
+    for layer in range(3):
+        edges.append((layer * layer_rows // (2 * share_rows), ((layer + 1) * layer_rows - 1) // (2 * share_rows)))
+
+    def ready(layer, at):
+        return max(abs(edge - at) for edges_of in edges[: layer + 1] for edge in edges_of)
+
+    for step in range(depth):
+        if step:
+            advance(share_line)
+            advance(third, fourth)
+
+            @pl.when(place >= step)
+            def _():
+                unpack(place - step)
+
+            @pl.when(place + step <= depth - 1)
+            def _():
+                unpack(place + step)
+
+        for layer in range(3):
+            places = [at for at in range(depth) if ready(layer, at) == step]
+            if places:
+                here = place == places[0]
+                for at in places[1:]:
+                    here = here | (place == at)
+
+                @pl.when(here)
+                def _():
+                    forward(layer)
+
+    begin = 2 * place * share_rows
+
+    def kernel_sums(layer, gradient):
+        for a in range(3):
+            low = (27 * layer + 9 * a) * channels
+
+            @pl.when((low + 9 * channels > begin) & (low < begin + 2 * share_rows))
+            def _():
+                sums = dot_rows(gradient[...], inputs_ref[layer, :, a * X : a * X + cells])
+                for c in range(3):
+                    block = sums[:, c * wide : (c + 1) * wide]
+                    parts = (
+                        block[channels:, :channels],
+                        block[:channels, :channels] + block[channels:, channels:],
+                        block[:channels, channels:],
+                    )
+                    for b in range(3):
+                        row = low + (3 * b + c) * channels
+                        square_ref[row : row + channels, :] = parts[b]
+
+    for layer in (2, 1):
+        held = grads_ref.at[2 - layer]
+        kernel_sums(layer, held.at[wide : 2 * wide, X : X + cells])
+
+        @pl.when(begin < layer * layer_rows)
+        def _():
+            @pl.loop(0, planes // 2)
+            def _(pair):
+                columns = pl.ds(pl.multiple_of(2 * pair * X, X), 2 * X)
+                total = convolved(back_ref.at[layer - 1], held, pair)
+                total = total * gelu_slope(pre_ref[layer - 1, :, columns])
+                if layer == 2:
+                    put(grads_ref.at[1], 2 * pair, total[:, :X])
+                    put(grads_ref.at[1], 2 * pair + 1, total[:, X:])
+                else:
+                    later = pl.ds(pl.multiple_of((2 * pair + 1) * X, X), 2 * X)
+                    grads_ref[0, wide : 2 * wide, later] = total.astype(jnp.bfloat16)
+
+    kernel_sums(0, grads_ref.at[0, wide : 2 * wide, X : X + cells])
+
+    while advance(share_line, third, fourth):
+        pass
+    made_ref[...] = made_all[pl.ds(place * own, own)]
+    sums = jnp.concatenate(
+        [
+            square_ref[pl.ds(begin, share_rows, stride=2), :],
+            square_ref[pl.ds(begin + 1, share_rows, stride=2), :],
+        ],
+        axis=1,
+    )
+
+    def adopted(mine, near):
+        return jnp.where(keep, mine, near.astype(jnp.float32)[:share_rows])
+
+    near = jnp.concatenate([moment_a[picks[0]], moment_b[picks[1]]], axis=0)
+    moment = momentum_decay * adopted(moment_ref[...], near) + sums
+    new_moment_ref[...] = moment
+    new_weight_ref[...] = adopted(weight_ref[...], kernels_ref[place]) - step_length * moment
+
+
+def on_device(trainers, depth, noise, gen_weight, gen_momentum, disc_weight, score_weight, pairing, flags):
+    own, channels = noise.shape[1], noise.shape[2]
+    planes = own * depth
+    if planes > WHOLE_PLANES or depth < 2 or trainers & (trainers - 1):
+        return on_device_split(
+            noise, gen_weight, gen_momentum, disc_weight, score_weight, pairing, flags
+        )
+    weight, moment = gen_weight.reshape(-1, X), gen_momentum.reshape(-1, X)
+    rows = weight.shape[0]
+    half = -(-rows // 32) * 16
+    levels = trainers.bit_length() - 1
+    wide = 2 * channels
+    framed = (planes + 2) * X
+    vmem = pl.BlockSpec(memory_space=pltpu.VMEM)
+    smem = pl.BlockSpec(memory_space=pltpu.SMEM)
+    slots = pltpu.VMEM((trainers, half, X), jnp.bfloat16)
+    made, new_weight, new_moment = pl.pallas_call(
+        functools.partial(round_kernel, trainers, depth),
+        out_shape=(
+            jax.ShapeDtypeStruct(noise.shape[1:], jnp.bfloat16),
+            jax.ShapeDtypeStruct(weight.shape, jnp.float32),
+            jax.ShapeDtypeStruct(weight.shape, jnp.float32),
+        ),
+        in_specs=[smem] * 2 + [vmem] * 5,
+        out_specs=(vmem,) * 3,
+        scratch_shapes=[
+            pltpu.VMEM((depth, 2 * half, X), jnp.bfloat16),
+            pltpu.VMEM((depth,) + noise.shape[1:], jnp.bfloat16),
+            slots,
+            slots,
+            slots,
+            slots,
+            pltpu.VMEM((81 * channels, channels), jnp.float32),
+            pltpu.VMEM((3, 3, wide, 3 * wide), jnp.bfloat16),
+            pltpu.VMEM((2, 3, wide, 3 * wide), jnp.bfloat16),
+            pltpu.VMEM((3, 3 * wide, framed), jnp.bfloat16),
+            pltpu.VMEM((2, 3 * wide, framed), jnp.bfloat16),
+            pltpu.VMEM((2, wide, planes * X), jnp.float32),
+            pltpu.VMEM((planes,) + noise.shape[2:], jnp.bfloat16),
+            pltpu.VMEM((X, 4 * wide), jnp.bfloat16),
+            pltpu.VMEM((2 * wide, 2 * X), jnp.bfloat16),
+            pltpu.SemaphoreType.DMA((4, levels)),
+            pltpu.SemaphoreType.DMA((4, levels)),
+            pltpu.SemaphoreType.DMA((8, depth - 1)),
+        ],
+        compiler_params=pltpu.CompilerParams(
+            collective_id=0, has_side_effects=True, vmem_limit_bytes=VMEM_LIMIT
+        ),
+    )(
+        pairing,
+        flags,
+        weight,
+        moment,
+        noise[0],
+        disc_weight[0].swapaxes(1, 2),
+        score_weight,
+    )
+    return made[None], new_weight.reshape(gen_weight.shape), new_moment.reshape(gen_weight.shape)
+
+
 def solution(mesh):
     placed = (
         P("trainer", "depth", None, None),
@@ -198,7 +670,7 @@
         P(),
     )
     return jax.shard_map(
-        on_device,
+        functools.partial(on_device, mesh.shape["trainer"], mesh.shape["depth"]),
         mesh=mesh,
         in_specs=placed,
         out_specs=(P("trainer", "depth", None, None), P("trainer", "depth"), P("trainer", "depth")),

time: 231 us -> 55.9 us (0.24)
  waiting for transfers between devices: 75.1 us -> 0 us
  Pallas kernels: 0 us -> 51 us
  local copies, waits for them, and re-layouts: 39.8 us -> 4.07 us
  starting transfers between devices: 28.2 us -> 0 us
  blocking collectives: 25.9 us -> 0 us
  matrix products: 23.3 us -> 0 us
  other arithmetic: 19.5 us -> 0 us
  between operations: 17.9 us -> 0.64 us
    pallas_call x0 -> x1, Pallas kernels: none -> 51 us  [on_device(): pl.pallas_call(functools.partial(round_kernel, trainers, depth), out_shap...]
    psum x1 -> x0, waiting for transfers between devices: 41.7 us -> none  [on_device(): lax.psum(local_grad.astype(jnp.bfloat16), 'depth').astype(jnp.float32)]
    all_gather x1 -> x0, blocking collectives: 25.9 us -> none  [on_device(): lax.all_gather(chosen_weight.astype(jnp.bfloat16), 'depth', axis=1, tiled...]
    dot_general x74 -> x0, matrix products: 23.3 us -> none  [the longest x45 11.4 us: convolve_grouped(): jnp.einsum('oj,zjs->zos', grouped[read_z, read_y], window[read_z:read_z +...]
    ppermute x10 -> x0, starting transfers between devices: 22.8 us -> none  [the longest x5 16 us: extended(): lax.ppermute(lax.slice_in_dim(block, block.shape[dim] - width, None, axis...]
    all_to_all x1 -> x0, waiting for transfers between devices: 21.7 us -> none  [on_device(): lax.all_to_all(outgoing.astype(jnp.bfloat16), 'trainer', split_axis=0, co...]
    another operation x34 -> x0, local copies, waits for them, and re-layouts: 14.3 us -> none
    ppermute x10 -> x0, waiting for transfers between devices: 11.6 us -> none  [the longest x5 11.6 us: extended(): lax.ppermute(lax.slice_in_dim(block, 0, width, axis=dim), axis, backward)]
  transfers between devices with their start and end apart: 12 -> 0, of which waited for: 7 -> 0; matrix products, arithmetic and copies ran while one was open for 4% -> 0% of each run, Pallas kernels for 0% -> 0%
where the time goes in v2:
time: 55.9 us; the launch traced here: 55.7 us
  Pallas kernels  51 us (91%)
  local copies, waits for them, and re-layouts  4.07 us (7%)
  between operations  0.64 us (1%)
    pallas_call x1, Pallas kernels, on_device(): pl.pallas_call(functools.partial(round_kernel, trainers, depth), out_shap...  51 us
    unnamed x5, local copies, waits for them, and re-layouts  4.07 us

profile of v2, /device:TPU:0, one launch (start us, length us, event | category | flops | bytes accessed | tf_op | source)
XLA Modules:
  0.0 55.7 jit_solution(9179196147098408313)
XLA Ops:
  0.6 51.0 %shard_map.94 = (bf16[4,64,256]{2,1,0:T(8,128)(2,1)}, f32[648,128]{1,0:T(8,128)}, f32[648,128]{1,0:T(8,128)}) custom-call(s32[8]{0:T(128)} %pairing_ref.1, s32[8]{0:T(128)} %flags_ref.1, f32[648,128]{1,0:T(8,128)} %bitcast.11, f32[648,128]{1,0:T(8,128)} %bitcast.12, bf16[4,64,256]{2,1,0:T(8,128)(2,1)} %bitcast.14, bf16[8,64,128]{2,1,0:T(8,128)(2,1)} %bitcast.15, ...), custom_call_target="tpu_custom_call" | custom-call | tf_op jit(solution)/shard_map/pallas_call | solution.py:618
  51.6 1.6 %copy.13 = bf16[1,4,64,256]{3,2,1,0:T(8,128)(2,1)} copy(bf16[1,4,64,256]{3,2,1,0:T(8,128)(2,1)} %bitcast.13) | data formatting | bytes 262144
  53.2 0.0 copy-start
  53.2 1.8 %copy.14 = f32[1,82944]{1,0:T(1,128)} copy(f32[1,82944]{1,0:T(1,128)} %bitcast.10) | data formatting | bytes 663552
  54.9 0.0 copy-done
  55.0 0.7 %copy.15 = f32[1,82944]{1,0:T(1,128)} copy(f32[1,82944]{1,0:T(1,128)S(1)} %bitcast.9) | data formatting | bytes 663552
Async XLA Ops:
  53.2 1.8 %copy-start = (f32[648,128]{1,0:T(8,128)S(1)}, f32[648,128]{1,0:T(8,128)}, u32[]{:S(2)}) copy-start(f32[648,128]{1,0:T(8,128)} %get-tuple-element.8) | copy-start | bytes 995332

commit v3 on v2

--- a/solution.py
+++ b/solution.py
@@ -192,7 +192,7 @@
 
 
 MESH = pl.DeviceIdType.MESH
-VMEM_LIMIT = 56 * 1024 * 1024
+VMEM_LIMIT = 32 * 1024 * 1024
 WHOLE_PLANES = 16
 
 
@@ -317,7 +317,8 @@
     made_ref,
     new_weight_ref,
     new_moment_ref,
-    kernels_ref,
+    kernels_a,
+    kernels_b,
     volume_ref,
     weight_a,
     weight_b,
@@ -376,9 +377,10 @@
     second = doubling(weight_b, order_b, rank, send_sem.at[1], recv_sem.at[1])
     third = doubling(moment_a, order_a, rank, send_sem.at[2], recv_sem.at[2])
     fourth = doubling(moment_b, order_b, rank, send_sem.at[3], recv_sem.at[3])
-    share_line = line_gather(
-        kernels_ref, place, depth, line_sem.at[4], line_sem.at[5], line_sem.at[6], line_sem.at[7]
-    )
+    share_lines = [
+        line_gather(slots, place, depth, *[line_sem.at[4 * k + j] for j in range(4)])
+        for k, slots in ((1, kernels_a), (2, kernels_b))
+    ]
     advance(first, second, noise_line)
 
     lane = lax.broadcasted_iota(jnp.int32, (wide, X), 1)
@@ -410,20 +412,23 @@
             differs = lax.rem(rank // bit + partner // bit, 2)
             pick = pick + differs * (1 << k)
         picks.append(jnp.where(keep, 0, pick))
-    kernels_ref[place, :half] = weight_a[picks[0]]
-    kernels_ref[place, half:] = weight_b[picks[1]]
-    advance(share_line, third, fourth)
+    kernels_a[place] = weight_a[picks[0]]
+    kernels_b[place] = weight_b[picks[1]]
+    advance(*share_lines, third, fourth)
 
     def put(buffer, plane, value):
-        columns = pl.ds(pl.multiple_of((plane + 1) * X, X), X)
+        columns = pl.ds((plane + 1) * X, X)
         low = jnp.where(lane == 0, 0.0, pltpu.roll(value, 1, 1))
         high = jnp.where(lane == X - 1, 0.0, pltpu.roll(value, X - 1, 1))
         buffer[0:wide, columns] = low.astype(jnp.bfloat16)
         buffer[wide : 2 * wide, columns] = value.astype(jnp.bfloat16)
         buffer[2 * wide : 3 * wide, columns] = high.astype(jnp.bfloat16)
 
+    def near_rows(low, high):
+        return jnp.concatenate([low, high], axis=0).astype(jnp.float32)[:share_rows]
+
     def unpack(part):
-        rows = kernels_ref[part].astype(jnp.float32)[:share_rows]
+        rows = near_rows(kernels_a[part], kernels_b[part])
         begin = pl.multiple_of(2 * part * share_rows, 8)
         square_ref[pl.ds(begin, share_rows, stride=2), :] = rows[:, :channels]
         square_ref[pl.ds(begin + 1, share_rows, stride=2), :] = rows[:, channels:]
@@ -452,7 +457,7 @@
     def convolved(weights, buffer, pair):
         total = None
         for a in range(3):
-            columns = pl.ds(pl.multiple_of((2 * pair + a) * X, X), 2 * X)
+            columns = pl.ds((2 * pair + a) * X, 2 * X)
             term = dot(weights[a], buffer[:, columns])
             total = term if total is None else total + term
         return total
@@ -460,11 +465,10 @@
     def forward(layer):
         prepare(layer)
 
-        @pl.loop(0, planes // 2)
-        def _(pair):
+        for pair in range(planes // 2):
             total = convolved(fore_ref.at[layer], inputs_ref.at[layer], pair)
             if layer < 2:
-                pre_ref[layer, :, pl.ds(pl.multiple_of(2 * pair * X, X), 2 * X)] = total
+                pre_ref[layer, :, 2 * pair * X : (2 * pair + 2) * X] = total
                 act = gelu_of(total)
                 put(inputs_ref.at[layer + 1], 2 * pair, act[:, :X])
                 put(inputs_ref.at[layer + 1], 2 * pair + 1, act[:, X:])
@@ -501,8 +505,7 @@
         pass
     for part in range(depth):
 
-        @pl.loop(0, own)
-        def _(plane):
+        for plane in range(own):
             both = volume_ref[part, plane].astype(jnp.float32)
             whole = jnp.concatenate([both[:, :X], both[:, X:]], axis=0)
             put(inputs_ref.at[0], part * own + plane, whole)
@@ -513,11 +516,13 @@
         edges.append((layer * layer_rows // (2 * share_rows), ((layer + 1) * layer_rows - 1) // (2 * share_rows)))
 
     def ready(layer, at):
-        return max(abs(edge - at) for edges_of in edges[: layer + 1] for edge in edges_of)
+        before = ready(layer - 1, at) if layer else 0
+        last = max(abs(edge - at) for edge in edges[layer])
+        return max(before, layer + 1 if last <= layer + 1 < depth else depth - 1)
 
     for step in range(depth):
         if step:
-            advance(share_line)
+            advance(*share_lines)
             advance(third, fourth)
 
             @pl.when(place >= step)
@@ -565,21 +570,20 @@
 
         @pl.when(begin < layer * layer_rows)
         def _():
-            @pl.loop(0, planes // 2)
-            def _(pair):
-                columns = pl.ds(pl.multiple_of(2 * pair * X, X), 2 * X)
+            for pair in range(planes // 2):
+                columns = pl.ds(2 * pair * X, 2 * X)
                 total = convolved(back_ref.at[layer - 1], held, pair)
                 total = total * gelu_slope(pre_ref[layer - 1, :, columns])
                 if layer == 2:
                     put(grads_ref.at[1], 2 * pair, total[:, :X])
                     put(grads_ref.at[1], 2 * pair + 1, total[:, X:])
                 else:
-                    later = pl.ds(pl.multiple_of((2 * pair + 1) * X, X), 2 * X)
+                    later = pl.ds((2 * pair + 1) * X, 2 * X)
                     grads_ref[0, wide : 2 * wide, later] = total.astype(jnp.bfloat16)
 
     kernel_sums(0, grads_ref.at[0, wide : 2 * wide, X : X + cells])
 
-    while advance(share_line, third, fourth):
+    while advance(*share_lines, third, fourth):
         pass
     made_ref[...] = made_all[pl.ds(place * own, own)]
     sums = jnp.concatenate(
@@ -591,12 +595,13 @@
     )
 
     def adopted(mine, near):
-        return jnp.where(keep, mine, near.astype(jnp.float32)[:share_rows])
-
-    near = jnp.concatenate([moment_a[picks[0]], moment_b[picks[1]]], axis=0)
-    moment = momentum_decay * adopted(moment_ref[...], near) + sums
+        return jnp.where(keep, mine, near)
+
+    near_moment = near_rows(moment_a[picks[0]], moment_b[picks[1]])
+    near_weight = near_rows(kernels_a[place], kernels_b[place])
+    moment = momentum_decay * adopted(moment_ref[...], near_moment) + sums
     new_moment_ref[...] = moment
-    new_weight_ref[...] = adopted(weight_ref[...], kernels_ref[place]) - step_length * moment
+    new_weight_ref[...] = adopted(weight_ref[...], near_weight) - step_length * moment
 
 
 def on_device(trainers, depth, noise, gen_weight, gen_momentum, disc_weight, score_weight, pairing, flags):
@@ -625,7 +630,8 @@
         in_specs=[smem] * 2 + [vmem] * 5,
         out_specs=(vmem,) * 3,
         scratch_shapes=[
-            pltpu.VMEM((depth, 2 * half, X), jnp.bfloat16),
+            pltpu.VMEM((depth, half, X), jnp.bfloat16),
+            pltpu.VMEM((depth, half, X), jnp.bfloat16),
             pltpu.VMEM((depth,) + noise.shape[1:], jnp.bfloat16),
             slots,
             slots,
@@ -642,7 +648,7 @@
             pltpu.VMEM((2 * wide, 2 * X), jnp.bfloat16),
             pltpu.SemaphoreType.DMA((4, levels)),
             pltpu.SemaphoreType.DMA((4, levels)),
-            pltpu.SemaphoreType.DMA((8, depth - 1)),
+            pltpu.SemaphoreType.DMA((12, depth - 1)),
         ],
         compiler_params=pltpu.CompilerParams(
             collective_id=0, has_side_effects=True, vmem_limit_bytes=VMEM_LIMIT

time: 55.9 us -> 48.2 us (0.86)
  Pallas kernels: 51 us -> 40.8 us
  local copies, waits for them, and re-layouts: 4.07 us -> 6.53 us
    pallas_call x1, Pallas kernels: 51 us -> 40.8 us  [on_device(): pl.pallas_call(functools.partial(round_kernel, trainers, depth), out_shap...]
    unnamed x5 -> x17, local copies, waits for them, and re-layouts: 4.07 us -> 6.53 us
where the time goes in v3:
time: 48.2 us; the launch traced here: 48 us
  Pallas kernels  40.8 us (85%)
  local copies, waits for them, and re-layouts  6.53 us (14%)
  between operations  0.67 us (1%)
    pallas_call x1, Pallas kernels, on_device(): pl.pallas_call(functools.partial(round_kernel, trainers, depth), out_shap...  40.8 us
    unnamed x17, local copies, waits for them, and re-layouts  6.53 us

profile of v3, /device:TPU:0, one launch (start us, length us, event | category | flops | bytes accessed | tf_op | source)
XLA Modules:
  0.0 48.0 jit_solution(7455396837164061586)
XLA Ops:
  0.6 0.0 copy-start.4
  0.6 0.0 copy-start.5
  0.7 0.0 copy-start.6
  0.7 0.6 %copy-done.4 = s32[8]{0:T(128)S(1)} copy-done((s32[8]{0:T(128)S(1)}, s32[8]{0:T(128)}, u32[]{:S(2)}) %copy-start.4) | copy-done | bytes 56
  1.3 0.0 copy-done.5
  1.3 0.0 copy-done.6
  1.3 0.0 copy-start
  1.3 1.0 %copy-done = f32[1,82944]{1,0:T(1,128)S(1)} copy-done((f32[1,82944]{1,0:T(1,128)S(1)}, f32[1,82944]{1,0:T(1,128)}, u32[]{:S(2)}) %copy-start) | copy-done | bytes 331800
  2.3 0.0 copy-start.1
  2.3 1.0 %copy-done.1 = f32[1,82944]{1,0:T(1,128)S(1)} copy-done((f32[1,82944]{1,0:T(1,128)S(1)}, f32[1,82944]{1,0:T(1,128)}, u32[]{:S(2)}) %copy-start.1) | copy-done | bytes 331800
  3.3 0.0 copy-start.2
  3.3 0.9 %copy-done.2 = bf16[1,4,64,256]{3,2,1,0:T(8,128)(2,1)S(1)} copy-done((bf16[1,4,64,256]{3,2,1,0:T(8,128)(2,1)S(1)}, bf16[1,4,64,256]{3,2,1,0:T(8,128)(2,1)}, u32[]{:S(2)}) %copy-start.2) | copy-done | bytes 131096
  4.2 0.0 copy-start.3
  4.2 0.9 %copy-done.3 = bf16[1,8,128,64]{2,3,1,0:T(8,128)(2,1)S(1)} copy-done((bf16[1,8,128,64]{2,3,1,0:T(8,128)(2,1)S(1)}, bf16[1,8,128,64]{2,3,1,0:T(8,128)(2,1)}, u32[]{:S(2)}) %copy-start.3) | copy-done | bytes 131096
  5.1 40.8 %shard_map.94 = (bf16[4,64,256]{2,1,0:T(8,128)(2,1)S(1)}, f32[648,128]{1,0:T(8,128)S(1)}, f32[648,128]{1,0:T(8,128)S(1)}) custom-call(s32[8]{0:T(128)S(1)} %copy-done.4, s32[8]{0:T(128)S(1)} %copy-done.5, f32[648,128]{1,0:T(8,128)S(1)} %bitcast.11, f32[648,128]{1,0:T(8,128)S(1)} %bitcast.12, bf16[4,64,256]{2,1,0:T(8,128)(2,1)S(1)} %bitcast.14, ...), custom_call_target="tpu_custom_call" | custom-call | tf_op jit(solution)/shard_map/pallas_call | solution.py:623
  45.9 0.7 %copy.13 = bf16[1,4,64,256]{3,2,1,0:T(8,128)(2,1)} copy(bf16[1,4,64,256]{3,2,1,0:T(8,128)(2,1)S(1)} %bitcast.13) | data formatting | bytes 262144
  46.5 0.7 %copy.14 = f32[1,82944]{1,0:T(1,128)} copy(f32[1,82944]{1,0:T(1,128)S(1)} %bitcast.10) | data formatting | bytes 663552
  47.2 0.7 %copy.15 = f32[1,82944]{1,0:T(1,128)} copy(f32[1,82944]{1,0:T(1,128)S(1)} %bitcast.9) | data formatting | bytes 663552
Async XLA Ops:
  0.6 0.7 %copy-start.4 = (s32[8]{0:T(128)S(1)}, s32[8]{0:T(128)}, u32[]{:S(2)}) copy-start(s32[8]{0:T(128)} %pairing_ref.1) | copy-start | bytes 100
  0.6 0.7 %copy-start.5 = (s32[8]{0:T(128)S(1)}, s32[8]{0:T(128)}, u32[]{:S(2)}) copy-start(s32[8]{0:T(128)} %flags_ref.1) | copy-start | bytes 100
  0.7 0.7 %copy-start.6 = (f32[1,128]{1,0:T(1,128)S(1)}, f32[1,128]{1,0:T(1,128)}, u32[]{:S(2)}) copy-start(f32[1,128]{1,0:T(1,128)} %score_ref.1) | copy-start | bytes 1540
  1.3 1.0 %copy-start = (f32[1,82944]{1,0:T(1,128)S(1)}, f32[1,82944]{1,0:T(1,128)}, u32[]{:S(2)}) copy-start(f32[1,82944]{1,0:T(1,128)} %param.8) | copy-start | bytes 995332
  2.3 1.0 %copy-start.1 = (f32[1,82944]{1,0:T(1,128)S(1)}, f32[1,82944]{1,0:T(1,128)}, u32[]{:S(2)}) copy-start(f32[1,82944]{1,0:T(1,128)} %param.9) | copy-start | bytes 995332
  3.3 0.9 %copy-start.2 = (bf16[1,4,64,256]{3,2,1,0:T(8,128)(2,1)S(1)}, bf16[1,4,64,256]{3,2,1,0:T(8,128)(2,1)}, u32[]{:S(2)}) copy-start(bf16[1,4,64,256]{3,2,1,0:T(8,128)(2,1)} %param.7) | copy-start | bytes 393220
  4.2 0.9 %copy-start.3 = (bf16[1,8,128,64]{2,3,1,0:T(8,128)(2,1)S(1)}, bf16[1,8,128,64]{2,3,1,0:T(8,128)(2,1)}, u32[]{:S(2)}) copy-start(bf16[1,8,128,64]{2,3,1,0:T(8,128)(2,1)} %param.10) | copy-start | bytes 393220

commit v4 on v3

--- a/solution.py
+++ b/solution.py
@@ -192,8 +192,9 @@
 
 
 MESH = pl.DeviceIdType.MESH
-VMEM_LIMIT = 32 * 1024 * 1024
+VMEM_LIMIT = 56 * 1024 * 1024
 WHOLE_PLANES = 16
+PIECES = 4
 
 
 def bit_orders(count):
@@ -309,19 +310,18 @@
     depth,
     pairing_ref,
     flags_ref,
-    weight_ref,
-    moment_ref,
-    noise_ref,
-    disc_ref,
+    weight_hbm,
+    moment_hbm,
+    noise_hbm,
+    disc_hbm,
     score_ref,
     made_ref,
     new_weight_ref,
     new_moment_ref,
-    kernels_a,
-    kernels_b,
+    weight_ref,
+    moment_ref,
+    disc_ref,
     volume_ref,
-    weight_a,
-    weight_b,
     moment_a,
     moment_b,
     square_ref,
@@ -333,11 +333,14 @@
     made_all,
     critic_ref,
     critic_back_ref,
+    load_sem,
     send_sem,
     recv_sem,
     line_sem,
+    *piece_refs,
 ):
-    own, channels = noise_ref.shape[0], noise_ref.shape[1]
+    slots, kernels = piece_refs[:PIECES], piece_refs[PIECES:]
+    own, channels = noise_hbm.shape[0], noise_hbm.shape[1]
     planes = own * depth
     wide = 2 * channels
     cells = planes * X
@@ -345,6 +348,20 @@
     rank = lax.axis_index("trainer")
     place = lax.axis_index("depth")
     order_a, order_b = bit_orders(trainers)
+    orders = (order_a, order_b) * (PIECES // 2)
+    loads = [
+        pltpu.make_async_copy(source, target, load_sem.at[k])
+        for k, (source, target) in enumerate(
+            (
+                (weight_hbm, weight_ref),
+                (noise_hbm, volume_ref.at[place]),
+                (disc_hbm, disc_ref),
+                (moment_hbm, moment_ref),
+            )
+        )
+    ]
+    for load in loads:
+        load.start()
     barrier = pltpu.get_barrier_semaphore()
     for bit in order_a:
         pl.semaphore_signal(
@@ -359,13 +376,20 @@
     def _():
         pl.semaphore_signal(barrier, inc=1, device_id={"depth": place + 1}, device_id_type=MESH)
 
-    half = weight_a.shape[1]
-    padding = jnp.zeros((2 * half - share_rows, weight_ref.shape[1]), jnp.float32)
-    weight_a[0] = weight_ref[:half].astype(jnp.bfloat16)
-    weight_b[0] = jnp.concatenate([weight_ref[half:], padding], axis=0).astype(jnp.bfloat16)
-    moment_a[0] = moment_ref[:half].astype(jnp.bfloat16)
-    moment_b[0] = jnp.concatenate([moment_ref[half:], padding], axis=0).astype(jnp.bfloat16)
-    volume_ref[place] = noise_ref[...]
+    def cut(source, begin, rows):
+        piece = source[begin : min(begin + rows, share_rows)]
+        lack = rows - piece.shape[0]
+        if lack:
+            padding = jnp.zeros((lack, piece.shape[1]), jnp.float32)
+            piece = jnp.concatenate([piece, padding], axis=0)
+        return piece.astype(jnp.bfloat16)
+
+    loads[0].wait()
+    begin = 0
+    for piece in slots:
+        piece[0] = cut(weight_ref, begin, piece.shape[1])
+        begin += piece.shape[1]
+    loads[1].wait()
 
     beside = (place > 0).astype(jnp.int32) + (place < depth - 1).astype(jnp.int32)
     pl.semaphore_wait(barrier, len(order_a) + beside)
@@ -373,15 +397,19 @@
     noise_line = line_gather(
         volume_ref, place, depth, line_sem.at[0], line_sem.at[1], line_sem.at[2], line_sem.at[3]
     )
-    first = doubling(weight_a, order_a, rank, send_sem.at[0], recv_sem.at[0])
-    second = doubling(weight_b, order_b, rank, send_sem.at[1], recv_sem.at[1])
-    third = doubling(moment_a, order_a, rank, send_sem.at[2], recv_sem.at[2])
-    fourth = doubling(moment_b, order_b, rank, send_sem.at[3], recv_sem.at[3])
+    near = [
+        doubling(piece, order, rank, send_sem.at[k], recv_sem.at[k])
+        for k, (piece, order) in enumerate(zip(slots, orders))
+    ]
+    third = doubling(moment_a, order_a, rank, send_sem.at[PIECES], recv_sem.at[PIECES])
+    fourth = doubling(moment_b, order_b, rank, send_sem.at[PIECES + 1], recv_sem.at[PIECES + 1])
     share_lines = [
-        line_gather(slots, place, depth, *[line_sem.at[4 * k + j] for j in range(4)])
-        for k, slots in ((1, kernels_a), (2, kernels_b))
+        line_gather(piece, place, depth, *[line_sem.at[4 * k + 4 + j] for j in range(4)])
+        for k, piece in enumerate(kernels)
     ]
-    advance(first, second, noise_line)
+    groups = [slice(k, k + 2) for k in range(0, PIECES, 2)]
+    advance(*near[groups[0]], noise_line)
+    loads[2].wait()
 
     lane = lax.broadcasted_iota(jnp.int32, (wide, X), 1)
     blocks = [
@@ -400,9 +428,6 @@
         buffer[:, 0:X] = empty
         buffer[:, cells + X : cells + 2 * X] = empty
 
-    while advance(first, second):
-        advance(noise_line)
-
     keep = flags_ref[rank] == 1
     partner = pairing_ref[rank]
     picks = []
@@ -412,9 +437,22 @@
             differs = lax.rem(rank // bit + partner // bit, 2)
             pick = pick + differs * (1 << k)
         picks.append(jnp.where(keep, 0, pick))
-    kernels_a[place] = weight_a[picks[0]]
-    kernels_b[place] = weight_b[picks[1]]
-    advance(*share_lines, third, fourth)
+    levels = len(order_a)
+    for tick in range(1, levels + len(groups)):
+        for k, group in enumerate(groups):
+            if 0 <= tick - k <= levels:
+                advance(*near[group])
+            if tick - k == levels:
+                for at in range(PIECES)[group]:
+                    kernels[at][place] = slots[at][picks[at % 2]]
+                advance(*share_lines[group])
+        if tick < levels + 1:
+            advance(noise_line)
+    loads[3].wait()
+    half = moment_a.shape[1]
+    moment_a[0] = cut(moment_ref, 0, half)
+    moment_b[0] = cut(moment_ref, half, half)
+    advance(third, fourth)
 
     def put(buffer, plane, value):
         columns = pl.ds((plane + 1) * X, X)
@@ -424,11 +462,11 @@
         buffer[wide : 2 * wide, columns] = value.astype(jnp.bfloat16)
         buffer[2 * wide : 3 * wide, columns] = high.astype(jnp.bfloat16)
 
-    def near_rows(low, high):
-        return jnp.concatenate([low, high], axis=0).astype(jnp.float32)[:share_rows]
+    def near_rows(*rows):
+        return jnp.concatenate(rows, axis=0).astype(jnp.float32)[:share_rows]
 
     def unpack(part):
-        rows = near_rows(kernels_a[part], kernels_b[part])
+        rows = near_rows(*[piece[part] for piece in kernels])
         begin = pl.multiple_of(2 * part * share_rows, 8)
         square_ref[pl.ds(begin, share_rows, stride=2), :] = rows[:, :channels]
         square_ref[pl.ds(begin + 1, share_rows, stride=2), :] = rows[:, channels:]
@@ -463,8 +501,6 @@
         return total
 
     def forward(layer):
-        prepare(layer)
-
         for pair in range(planes // 2):
             total = convolved(fore_ref.at[layer], inputs_ref.at[layer], pair)
             if layer < 2:
@@ -515,9 +551,12 @@
     for layer in range(3):
         edges.append((layer * layer_rows // (2 * share_rows), ((layer + 1) * layer_rows - 1) // (2 * share_rows)))
 
+    def known(layer, at):
+        return max(abs(edge - at) for edge in edges[layer])
+
     def ready(layer, at):
         before = ready(layer - 1, at) if layer else 0
-        last = max(abs(edge - at) for edge in edges[layer])
+        last = known(layer, at)
         return max(before, layer + 1 if last <= layer + 1 < depth else depth - 1)
 
     for step in range(depth):
@@ -533,16 +572,17 @@
             def _():
                 unpack(place + step)
 
-        for layer in range(3):
-            places = [at for at in range(depth) if ready(layer, at) == step]
-            if places:
-                here = place == places[0]
-                for at in places[1:]:
-                    here = here | (place == at)
-
-                @pl.when(here)
-                def _():
-                    forward(layer)
+        for act, due in ((prepare, known), (forward, ready)):
+            for layer in range(3):
+                places = [at for at in range(depth) if due(layer, at) == step]
+                if places:
+                    here = place == places[0]
+                    for at in places[1:]:
+                        here = here | (place == at)
+
+                    @pl.when(here)
+                    def _():
+                        act(layer)
 
     begin = 2 * place * share_rows
 
@@ -598,7 +638,7 @@
         return jnp.where(keep, mine, near)
 
     near_moment = near_rows(moment_a[picks[0]], moment_b[picks[1]])
-    near_weight = near_rows(kernels_a[place], kernels_b[place])
+    near_weight = near_rows(*[piece[place] for piece in kernels])
     moment = momentum_decay * adopted(moment_ref[...], near_moment) + sums
     new_moment_ref[...] = moment
     new_weight_ref[...] = adopted(weight_ref[...], near_weight) - step_length * moment
@@ -614,12 +654,15 @@
     weight, moment = gen_weight.reshape(-1, X), gen_momentum.reshape(-1, X)
     rows = weight.shape[0]
     half = -(-rows // 32) * 16
+    units = -(-rows // 16)
+    sizes = [16 * ((units + PIECES - 1 - k) // PIECES) for k in range(PIECES)]
     levels = trainers.bit_length() - 1
     wide = 2 * channels
     framed = (planes + 2) * X
     vmem = pl.BlockSpec(memory_space=pltpu.VMEM)
     smem = pl.BlockSpec(memory_space=pltpu.SMEM)
-    slots = pltpu.VMEM((trainers, half, X), jnp.bfloat16)
+    hbm = pl.BlockSpec(memory_space=pltpu.HBM)
+    moments = pltpu.VMEM((trainers, half, X), jnp.bfloat16)
     made, new_weight, new_moment = pl.pallas_call(
         functools.partial(round_kernel, trainers, depth),
         out_shape=(
@@ -627,16 +670,15 @@
             jax.ShapeDtypeStruct(weight.shape, jnp.float32),
             jax.ShapeDtypeStruct(weight.shape, jnp.float32),
         ),
-        in_specs=[smem] * 2 + [vmem] * 5,
+        in_specs=[smem] * 2 + [hbm] * 4 + [vmem],
         out_specs=(vmem,) * 3,
         scratch_shapes=[
-            pltpu.VMEM((depth, half, X), jnp.bfloat16),
-            pltpu.VMEM((depth, half, X), jnp.bfloat16),
+            pltpu.VMEM(weight.shape, jnp.float32),
+            pltpu.VMEM(weight.shape, jnp.float32),
+            pltpu.VMEM((8, channels, X), jnp.bfloat16),
             pltpu.VMEM((depth,) + noise.shape[1:], jnp.bfloat16),
-            slots,
-            slots,
-            slots,
-            slots,
+            moments,
+            moments,
             pltpu.VMEM((81 * channels, channels), jnp.float32),
             pltpu.VMEM((3, 3, wide, 3 * wide), jnp.bfloat16),
             pltpu.VMEM((2, 3, wide, 3 * wide), jnp.bfloat16),
@@ -646,10 +688,13 @@
             pltpu.VMEM((planes,) + noise.shape[2:], jnp.bfloat16),
             pltpu.VMEM((X, 4 * wide), jnp.bfloat16),
             pltpu.VMEM((2 * wide, 2 * X), jnp.bfloat16),
-            pltpu.SemaphoreType.DMA((4, levels)),
-            pltpu.SemaphoreType.DMA((4, levels)),
-            pltpu.SemaphoreType.DMA((12, depth - 1)),
-        ],
+            pltpu.SemaphoreType.DMA((4,)),
+            pltpu.SemaphoreType.DMA((PIECES + 2, levels)),
+            pltpu.SemaphoreType.DMA((PIECES + 2, levels)),
+            pltpu.SemaphoreType.DMA((4 * PIECES + 4, depth - 1)),
+        ]
+        + [pltpu.VMEM((trainers, size, X), jnp.bfloat16) for size in sizes]
+        + [pltpu.VMEM((depth, size, X), jnp.bfloat16) for size in sizes],
         compiler_params=pltpu.CompilerParams(
             collective_id=0, has_side_effects=True, vmem_limit_bytes=VMEM_LIMIT
         ),

time: 48.2 us -> 46.7 us (0.969)
  local copies, waits for them, and re-layouts: 6.53 us -> 4.07 us
  Pallas kernels: 40.8 us -> 41.8 us
    unnamed x17 -> x5, local copies, waits for them, and re-layouts: 6.53 us -> 4.07 us
    pallas_call x1, Pallas kernels: 40.8 us -> 41.8 us  [on_device(): pl.pallas_call(functools.partial(round_kernel, trainers, depth), out_shap...]
where the time goes in v4:
time: 46.7 us; the launch traced here: 46.5 us
  Pallas kernels  41.8 us (90%)
  local copies, waits for them, and re-layouts  4.07 us (9%)
  between operations  0.64 us (1%)
    pallas_call x1, Pallas kernels, on_device(): pl.pallas_call(functools.partial(round_kernel, trainers, depth), out_shap...  41.8 us
    unnamed x5, local copies, waits for them, and re-layouts  4.07 us

profile of v4, /device:TPU:0, one launch (start us, length us, event | category | flops | bytes accessed | tf_op | source)
XLA Modules:
  0.0 46.5 jit_solution(7050382806762148155)
XLA Ops:
  0.6 41.8 %shard_map.94 = (bf16[4,64,256]{2,1,0:T(8,128)(2,1)}, f32[648,128]{1,0:T(8,128)}, f32[648,128]{1,0:T(8,128)}) custom-call(s32[8]{0:T(128)} %pairing_ref.1, s32[8]{0:T(128)} %flags_ref.1, f32[648,128]{1,0:T(8,128)} %bitcast.11, f32[648,128]{1,0:T(8,128)} %bitcast.12, bf16[4,64,256]{2,1,0:T(8,128)(2,1)} %bitcast.14, bf16[8,64,128]{2,1,0:T(8,128)(2,1)} %bitcast.15, ...), custom_call_target="tpu_custom_call" | custom-call | tf_op jit(solution)/shard_map/pallas_call | solution.py:666
  42.4 1.6 %copy.13 = bf16[1,4,64,256]{3,2,1,0:T(8,128)(2,1)} copy(bf16[1,4,64,256]{3,2,1,0:T(8,128)(2,1)} %bitcast.13) | data formatting | bytes 262144
  44.0 0.0 copy-start
  44.0 1.8 %copy.14 = f32[1,82944]{1,0:T(1,128)} copy(f32[1,82944]{1,0:T(1,128)} %bitcast.10) | data formatting | bytes 663552
  45.7 0.0 copy-done
  45.7 0.7 %copy.15 = f32[1,82944]{1,0:T(1,128)} copy(f32[1,82944]{1,0:T(1,128)S(1)} %bitcast.9) | data formatting | bytes 663552
Async XLA Ops:
  44.0 1.8 %copy-start = (f32[648,128]{1,0:T(8,128)S(1)}, f32[648,128]{1,0:T(8,128)}, u32[]{:S(2)}) copy-start(f32[648,128]{1,0:T(8,128)} %get-tuple-element.8) | copy-start | bytes 995332

commit v5 on v4

--- a/solution.py
+++ b/solution.py
@@ -666,9 +666,9 @@
     made, new_weight, new_moment = pl.pallas_call(
         functools.partial(round_kernel, trainers, depth),
         out_shape=(
-            jax.ShapeDtypeStruct(noise.shape[1:], jnp.bfloat16),
-            jax.ShapeDtypeStruct(weight.shape, jnp.float32),
-            jax.ShapeDtypeStruct(weight.shape, jnp.float32),
+            pltpu.VMEM(noise.shape[1:], jnp.bfloat16),
+            pltpu.VMEM(weight.shape, jnp.float32),
+            pltpu.VMEM(weight.shape, jnp.float32),
         ),
         in_specs=[smem] * 2 + [hbm] * 4 + [vmem],
         out_specs=(vmem,) * 3,

time: 46.7 us -> 43.8 us (0.938)
  local copies, waits for them, and re-layouts: 4.07 us -> 2.11 us
  Pallas kernels: 41.8 us -> 40.9 us
    unnamed x5 -> x3, local copies, waits for them, and re-layouts: 4.07 us -> 2.11 us
    pallas_call x1, Pallas kernels: 41.8 us -> 40.9 us  [on_device(): pl.pallas_call(functools.partial(round_kernel, trainers, depth), out_shap...]
where the time goes in v5:
time: 43.8 us; the launch traced here: 43.7 us
  Pallas kernels  40.9 us (93%)
  local copies, waits for them, and re-layouts  2.11 us (5%)
  between operations  0.64 us (1%)
    pallas_call x1, Pallas kernels, on_device(): pl.pallas_call(functools.partial(round_kernel, trainers, depth), out_shap...  40.9 us
    unnamed x3, local copies, waits for them, and re-layouts  2.11 us

profile of v5, /device:TPU:0, one launch (start us, length us, event | category | flops | bytes accessed | tf_op | source)
XLA Modules:
  0.0 43.7 jit_solution(8054766130861669506)
XLA Ops:
  0.6 40.9 %shard_map.94 = (bf16[4,64,256]{2,1,0:T(8,128)(2,1)S(1)}, f32[648,128]{1,0:T(8,128)S(1)}, f32[648,128]{1,0:T(8,128)S(1)}) custom-call(s32[8]{0:T(128)} %pairing_ref.1, s32[8]{0:T(128)} %flags_ref.1, f32[648,128]{1,0:T(8,128)} %bitcast.12, f32[648,128]{1,0:T(8,128)} %bitcast.13, bf16[4,64,256]{2,1,0:T(8,128)(2,1)} %bitcast.14, bf16[8,64,128]{2,1,0:T(8,128)(2,1)} %bitcast.15, ...), custom_call_target="tpu_custom_call" | custom-call | tf_op jit(solution)/shard_map/pallas_call | solution.py:666
  41.5 0.7 %copy.13 = bf16[1,4,64,256]{3,2,1,0:T(8,128)(2,1)} copy(bf16[1,4,64,256]{3,2,1,0:T(8,128)(2,1)S(1)} %bitcast.11) | data formatting | bytes 262144
  42.2 0.7 %copy.14 = f32[1,82944]{1,0:T(1,128)} copy(f32[1,82944]{1,0:T(1,128)S(1)} %bitcast.10) | data formatting | bytes 663552
  42.9 0.7 %copy.15 = f32[1,82944]{1,0:T(1,128)} copy(f32[1,82944]{1,0:T(1,128)S(1)} %bitcast.9) | data formatting | bytes 663552
